TPU v7x, 512 devices: a whole 4x8x8 slice. The times are simulated.
512 devices in a mesh: pp: 16 (over z_lo, x), ep: 32 (over z_hi, y, core).
Axes of the slice: x: 4, y: 8, z: 8 (z_hi: 2, z_lo: 4; z = z_hi * 4 + z_lo), core: 2. Of those that a mesh axis runs over, the one named last changes fastest.
Arguments:
- rising_state: bfloat16 [16, 2048, 3584], P('pp', 'ep'), may hold values from -6 to 6
- falling_state: bfloat16 [16, 2048, 3584], P('pp', 'ep'), may hold values from -6 to 6
- rising_ids: int32 [3, 16, 2048, 8], P(None, 'pp', 'ep'), may hold values from 0 to 255, all different within a row; in each aligned block of 64 rows (0 to 63, 64 to 127, ..., all dimensions but the last counted through in order) at most 4 rows name the same one
- falling_ids: int32 [3, 16, 2048, 8], P(None, 'pp', 'ep'), may hold values from 0 to 255, all different within a row; in each aligned block of 64 rows (0 to 63, 64 to 127, ..., all dimensions but the last counted through in order) at most 4 rows name the same one
- norm_gain: float32 [16, 3584], P('pp'), may hold values from 0.1 to 1.9
- router: bfloat16 [16, 256, 3584], P('pp', 'ep'), may hold values from -0.09375 to 0.09375
- w_gate: bfloat16 [16, 3584, 4096], P('pp', None, 'ep'), may hold values from -0.09375 to 0.09375
- w_up: bfloat16 [16, 3584, 4096], P('pp', None, 'ep'), may hold values from -0.09375 to 0.09375
- w_down: bfloat16 [16, 4096, 3584], P('pp', 'ep'), may hold values from -0.1875 to 0.1875
Outputs:
- rising_out: bfloat16 [16, 2048, 3584], P('pp', 'ep')
- falling_out: bfloat16 [16, 2048, 3584], P('pp', 'ep')
Inputs may be any that keep to these rules, and one draw needn't show every extreme that they name: `rising_ids`: each row names 8 different experts; within one step and rank, the 64 rows of one device name no expert more than 4 times. `falling_ids`: each row names 8 different experts; within one step and rank, the 64 rows of one device name no expert more than 4 times.
All inputs are finite; a program needn't handle non-finite values.
Results may differ from a plain program's by a relative error of at most 0.002.
Values may be sent and summed in bfloat16 or wider, within the bound.
A program may use at most 64 MiB of HBM per device.

v0:
```python
import jax
import jax.numpy as jnp
from jax import lax
from jax.sharding import PartitionSpec as P

SPLIT = 8
STEPS = 3
CAP = 4


route_scale = 2.5
norm_eps = 1e-06


def shifted(block, axis, distance):
    devices = range(lax.axis_size(axis))
    route = [((i - distance) % len(devices), i) for i in devices]
    return lax.ppermute(block, axis, route)


def prepare_layer(states, expert_ids, norm_gain, router_all, experts_here):
    values = states.astype(jnp.float32)
    inverse = lax.rsqrt(jnp.mean(values * values, axis=-1, keepdims=True) + norm_eps)
    normed = (values * inverse * norm_gain).astype(jnp.bfloat16)
    logits = lax.dot_general(
        normed, router_all, (((1,), (1,)), ((), ())), preferred_element_type=jnp.float32
    )
    columns = jnp.arange(router_all.shape[0], dtype=jnp.int32)
    picked = jnp.sum(
        jnp.where(expert_ids[:, :, None] == columns[None, None, :], logits[:, None, :], 0.0),
        axis=-1,
    )
    affinity = jax.nn.sigmoid(picked)
    gate_weights = route_scale * affinity / jnp.sum(affinity, axis=-1, keepdims=True)
    flat_ids = expert_ids.reshape(-1)
    window = jnp.arange(experts_here, dtype=jnp.int32)
    onehot = (flat_ids[:, None] == window[None, :]).astype(jnp.int32)
    earlier = jnp.cumsum(onehot, axis=0) - onehot
    slot_index = jnp.sum(onehot * earlier, axis=-1)
    target = jnp.where(flat_ids < experts_here, flat_ids * CAP + slot_index, -1).reshape(
        expert_ids.shape
    )
    slot_ids = jnp.arange(experts_here * CAP, dtype=jnp.int32)
    matched = target[:, :, None] == slot_ids[None, None, :]
    combine = jnp.sum(jnp.where(matched, gate_weights[:, :, None], 0.0), axis=1)
    dispatch = jnp.sum(matched.astype(jnp.float32), axis=1).astype(jnp.bfloat16)
    packed = lax.dot_general(
        dispatch, normed, (((0,), (0,)), ((), ())), preferred_element_type=jnp.float32
    ).astype(jnp.bfloat16)
    return (combine, packed.reshape(experts_here, CAP, normed.shape[1]))


def expert_apply(token_rows, w_gate, w_up, w_down):
    row_shape = token_rows.shape
    flat_rows = token_rows.reshape(-1, row_shape[-1])
    gate_out = jnp.dot(flat_rows, w_gate, preferred_element_type=jnp.float32)
    up_out = jnp.dot(flat_rows, w_up, preferred_element_type=jnp.float32)
    hidden = (jax.nn.silu(gate_out) * up_out).astype(jnp.bfloat16)
    partial_out = jnp.dot(hidden, w_down, preferred_element_type=jnp.float32).astype(jnp.bfloat16)
    return partial_out.reshape(row_shape)


def send_rows(packed_list, weights):
    copies = tuple((jnp.repeat(packed, SPLIT, axis=0) for packed in packed_list))
    received = (lax.all_to_all(copies[0], "ep", split_axis=0, concat_axis=0, tiled=True),)
    return tuple((expert_apply(received_block, *weights) for received_block in received))


def return_rows(partials):
    return (lax.all_to_all(partials[0], "ep", split_axis=0, concat_axis=0, tiled=True),)


def finish_layer(states, combine, returned, experts_here):
    model_width = states.shape[1]
    summed = returned.astype(jnp.float32).reshape(experts_here, SPLIT, CAP, model_width).sum(axis=1)
    summed = summed.reshape(experts_here * CAP, model_width)
    combined = jnp.dot(
        combine, summed, precision=lax.Precision.HIGHEST, preferred_element_type=jnp.float32
    )
    return (states.astype(jnp.float32) + combined).astype(jnp.bfloat16)


def move_rising(states):
    return shifted(states, "pp", 1)


def move_falling(states):
    return shifted(states, "pp", -1)


def body(
    rising_state, falling_state, rising_ids, falling_ids, norm_gain, router, w_gate, w_up, w_down
):
    router_all = lax.all_gather(router[0], "ep", axis=0, tiled=True)
    weights = (w_gate[0], w_up[0], w_down[0])
    experts_here = lax.axis_size("ep") // SPLIT
    layer_gain = norm_gain[0]
    rising = rising_state[0]
    falling = falling_state[0]
    for step_index in range(STEPS):
        plan_rise = prepare_layer(
            rising, rising_ids[step_index, 0], layer_gain, router_all, experts_here
        )
        plan_fall = prepare_layer(
            falling, falling_ids[step_index, 0], layer_gain, router_all, experts_here
        )
        partials = send_rows((plan_rise[1],), weights) + send_rows((plan_fall[1],), weights)
        returned = return_rows((partials[0],)) + return_rows((partials[1],))
        rising = move_rising(finish_layer(rising, plan_rise[0], returned[0], experts_here))
        falling = move_falling(finish_layer(falling, plan_fall[0], returned[1], experts_here))
    return (rising[None], falling[None])


def solution(mesh):
    return jax.shard_map(
        body,
        mesh=mesh,
        in_specs=(
            P("pp", "ep", None),
            P("pp", "ep", None),
            P(None, "pp", "ep", None),
            P(None, "pp", "ep", None),
            P("pp", None),
            P("pp", "ep", None),
            P("pp", None, "ep"),
            P("pp", None, "ep"),
            P("pp", "ep", None),
        ),
        out_specs=(P("pp", "ep", None), P("pp", "ep", None)),
        check_vma=False,
    )
```

profile of v0, /device:TPU:76, one launch (start us, length us, event | category | flops | bytes accessed | tf_op | source)
XLA Modules:
  0.0 592.2 jit_solution(10093616760043026575)
XLA Ops:
  16.7 87.5 %all-gather.3.cloned.1.call-done = bf16[1,256,3584]{2,1,0:T(8,128)(2,1)} async-done(((bf16[1,8,3584]{2,1,0:T(8,128)(2,1)}), bf16[1,256,3584]{2,1,0:T(8,128)(2,1)}) %all-gather.3.cloned.1.call-update) | async-done | bytes 1835024 | tf_op jit(solution)/shard_map/all_gather | solution.py:94
  109.0 7.6 %all-to-all-start.6 = ((bf16[32,4,3584]{2,1,0:T(4,128)(2,1)}), bf16[32,4,3584]{2,1,0:T(4,128)(2,1)}, u32[]{:S(2)}, u32[]{:S(2)}) async-start(bf16[32,4,3584]{2,1,0:T(4,128)(2,1)} %bitcast.280), calls=%async_computation.6 | async-start | bytes 1835008 | tf_op jit(solution)/shard_map/all_to_all | solution.py:65
  122.2 24.7 %all-to-all-done.6 = bf16[32,4,3584]{2,1,0:T(4,128)(2,1)} async-done(((bf16[32,4,3584]{2,1,0:T(4,128)(2,1)}), bf16[32,4,3584]{2,1,0:T(4,128)(2,1)}, u32[]{:S(2)}, u32[]{:S(2)}) %all-to-all-start.6) | async-done | bytes 917536 | tf_op jit(solution)/shard_map/all_to_all | solution.py:65
  148.0 4.4 all-to-all-start
  156.7 3.1 convolution_convert_fusion.2
  162.4 20.1 %all-to-all-done = bf16[32,4,3584]{2,1,0:T(4,128)(2,1)} async-done(((bf16[32,4,3584]{2,1,0:T(4,128)(2,1)}), bf16[32,4,3584]{2,1,0:T(4,128)(2,1)}, u32[]{:S(2)}, u32[]{:S(2)}) %all-to-all-start) | async-done | bytes 917536 | tf_op jit(solution)/shard_map/all_to_all | solution.py:65
  182.5 4.4 all-to-all-start.7
  191.4 3.1 convolution_convert_fusion.5
  197.0 20.0 %all-to-all-done.7 = bf16[32,4,3584]{2,1,0:T(4,128)(2,1)} async-done(((bf16[32,4,3584]{2,1,0:T(4,128)(2,1)}), bf16[32,4,3584]{2,1,0:T(4,128)(2,1)}, u32[]{:S(2)}, u32[]{:S(2)}) %all-to-all-start.7) | async-done | bytes 917536 | tf_op jit(solution)/shard_map/all_to_all | solution.py:70
  217.0 4.4 all-to-all-start.1
  237.0 14.5 %all-to-all-done.1 = bf16[32,4,3584]{2,1,0:T(4,128)(2,1)} async-done(((bf16[32,4,3584]{2,1,0:T(4,128)(2,1)}), bf16[32,4,3584]{2,1,0:T(4,128)(2,1)}, u32[]{:S(2)}, u32[]{:S(2)}) %all-to-all-start.1) | async-done | bytes 917536 | tf_op jit(solution)/shard_map/all_to_all | solution.py:70
  257.2 3.1 collective-permute-start
  266.7 4.4 all-to-all-start.8
  273.6 27.6 %all-to-all-done.8 = bf16[32,4,3584]{2,1,0:T(4,128)(2,1)} async-done(((bf16[32,4,3584]{2,1,0:T(4,128)(2,1)}), bf16[32,4,3584]{2,1,0:T(4,128)(2,1)}, u32[]{:S(2)}, u32[]{:S(2)}) %all-to-all-start.8) | async-done | bytes 917536 | tf_op jit(solution)/shard_map/all_to_all | solution.py:65
  302.3 4.4 all-to-all-start.2
  311.0 3.1 convolution_convert_fusion.1
  316.6 20.1 %all-to-all-done.2 = bf16[32,4,3584]{2,1,0:T(4,128)(2,1)} async-done(((bf16[32,4,3584]{2,1,0:T(4,128)(2,1)}), bf16[32,4,3584]{2,1,0:T(4,128)(2,1)}, u32[]{:S(2)}, u32[]{:S(2)}) %all-to-all-start.2) | async-done | bytes 917536 | tf_op jit(solution)/shard_map/all_to_all | solution.py:65
  336.8 4.4 all-to-all-start.9
  345.6 3.1 convolution_convert_fusion.4
  351.3 19.9 %all-to-all-done.9 = bf16[32,4,3584]{2,1,0:T(4,128)(2,1)} async-done(((bf16[32,4,3584]{2,1,0:T(4,128)(2,1)}), bf16[32,4,3584]{2,1,0:T(4,128)(2,1)}, u32[]{:S(2)}, u32[]{:S(2)}) %all-to-all-start.9) | async-done | bytes 917536 | tf_op jit(solution)/shard_map/all_to_all | solution.py:70
  371.2 4.6 all-to-all-start.3
  391.7 14.1 %all-to-all-done.3 = bf16[32,4,3584]{2,1,0:T(4,128)(2,1)} async-done(((bf16[32,4,3584]{2,1,0:T(4,128)(2,1)}), bf16[32,4,3584]{2,1,0:T(4,128)(2,1)}, u32[]{:S(2)}, u32[]{:S(2)}) %all-to-all-start.3) | async-done | bytes 917536 | tf_op jit(solution)/shard_map/all_to_all | solution.py:70
  411.6 12.2 %collective-permute-start.1 = (bf16[64,3584]{1,0:T(8,128)(2,1)}, bf16[64,3584]{1,0:T(8,128)(2,1)S(1)}, u32[]{:S(2)}, u32[]{:S(2)}) collective-permute-start(bf16[64,3584]{1,0:T(8,128)(2,1)} %fusion.1), channel_id=1, source_target_pairs={{480,0},{0,32},{32,64},{64,96},{96,128},{128,160},{160,192},{192,2... | collective-permute-start | bytes 1376264 | tf_op jit(solution)/shard_map/ppermute | solution.py:18
  429.7 4.4 all-to-all-start.10
  435.9 28.2 %all-to-all-done.10 = bf16[32,4,3584]{2,1,0:T(4,128)(2,1)} async-done(((bf16[32,4,3584]{2,1,0:T(4,128)(2,1)}), bf16[32,4,3584]{2,1,0:T(4,128)(2,1)}, u32[]{:S(2)}, u32[]{:S(2)}) %all-to-all-start.10) | async-done | bytes 917536 | tf_op jit(solution)/shard_map/all_to_all | solution.py:65
  465.4 4.6 all-to-all-start.4
  479.4 20.7 %all-to-all-done.4 = bf16[32,4,3584]{2,1,0:T(4,128)(2,1)} async-done(((bf16[32,4,3584]{2,1,0:T(4,128)(2,1)}), bf16[32,4,3584]{2,1,0:T(4,128)(2,1)}, u32[]{:S(2)}, u32[]{:S(2)}) %all-to-all-start.4) | async-done | bytes 917536 | tf_op jit(solution)/shard_map/all_to_all | solution.py:65
  500.1 4.4 all-to-all-start.11
  511.5 23.1 %all-to-all-done.11 = bf16[32,4,3584]{2,1,0:T(4,128)(2,1)} async-done(((bf16[32,4,3584]{2,1,0:T(4,128)(2,1)}), bf16[32,4,3584]{2,1,0:T(4,128)(2,1)}, u32[]{:S(2)}, u32[]{:S(2)}) %all-to-all-start.11) | async-done | bytes 917536 | tf_op jit(solution)/shard_map/all_to_all | solution.py:70
  534.6 4.0 all-to-all-start.5
  544.9 23.5 %all-to-all-done.5 = bf16[32,4,3584]{2,1,0:T(4,128)(2,1)S(1)} async-done(((bf16[32,4,3584]{2,1,0:T(4,128)(2,1)}), bf16[32,4,3584]{2,1,0:T(4,128)(2,1)S(1)}, u32[]{:S(2)}, u32[]{:S(2)}) %all-to-all-start.5) | async-done | bytes 917536 | tf_op jit(solution)/shard_map/all_to_all | solution.py:70
  571.8 11.6 %collective-permute-done.2 = bf16[64,3584]{1,0:T(8,128)(2,1)S(1)} collective-permute-done((bf16[64,3584]{1,0:T(8,128)(2,1)S(1)}, bf16[64,3584]{1,0:T(8,128)(2,1)S(1)}, u32[]{:S(2)}, u32[]{:S(2)}) %collective-permute-start.2) | collective-permute-done | bytes 458784 | tf_op jit(solution)/shard_map/ppermute | solution.py:18
  (224 shorter events, 137.4 us)
Async XLA Ops:
  7.2 149.6 %copy-start = (bf16[1,128,3584]{2,1,0:T(8,128)(2,1)S(1)}, bf16[1,128,3584]{2,1,0:T(8,128)(2,1)}, u32[]{:S(2)}) copy-start(bf16[1,128,3584]{2,1,0:T(8,128)(2,1)} %param.17) | copy-start | bytes 2752516
  7.2 97.0 %all-gather.3.cloned.1.call-start = ((), (), s32[]{:S(2)}) async-start(), calls=%async_computation.12 | async-start | bytes 1892352 | tf_op jit(solution)/shard_map/all_gather | solution.py:94
  7.9 99.6 %copy-start.4 = (bf16[1,64,3584]{2,1,0:T(8,128)(2,1)S(1)}, bf16[1,64,3584]{2,1,0:T(8,128)(2,1)}, u32[]{:S(2)}) copy-start(bf16[1,64,3584]{2,1,0:T(8,128)(2,1)} %param.10) | copy-start | bytes 1376260
  107.8 10.3 %copy-start.1 = (bf16[1,256,3584]{2,1,0:T(8,128)(2,1)S(1)}, bf16[1,256,3584]{2,1,0:T(8,128)(2,1)}, u32[]{:S(2)}) copy-start(bf16[1,256,3584]{2,1,0:T(8,128)(2,1)} %all-gather.3.cloned.1.call-done) | copy-start | bytes 5505028
  109.0 37.8 %all-to-all-start.6 = ((bf16[32,4,3584]{2,1,0:T(4,128)(2,1)}), bf16[32,4,3584]{2,1,0:T(4,128)(2,1)}, u32[]{:S(2)}, u32[]{:S(2)}) async-start(bf16[32,4,3584]{2,1,0:T(4,128)(2,1)} %bitcast.280), calls=%async_computation.6 | async-start | bytes 1835008 | tf_op jit(solution)/shard_map/all_to_all | solution.py:65
  148.0 34.5 %all-to-all-start = ((bf16[32,4,3584]{2,1,0:T(4,128)(2,1)}), bf16[32,4,3584]{2,1,0:T(4,128)(2,1)}, u32[]{:S(2)}, u32[]{:S(2)}) async-start(bf16[32,4,3584]{2,1,0:T(4,128)(2,1)} %bitcast.281), calls=%async_computation | async-start | bytes 1835008 | tf_op jit(solution)/shard_map/all_to_all | solution.py:65
  182.5 34.4 %all-to-all-start.7 = ((bf16[32,4,3584]{2,1,0:T(4,128)(2,1)}), bf16[32,4,3584]{2,1,0:T(4,128)(2,1)}, u32[]{:S(2)}, u32[]{:S(2)}) async-start(bf16[32,4,3584]{2,1,0:T(4,128)(2,1)} %reshape.552), calls=%async_computation.7 | async-start | bytes 1835008 | tf_op jit(solution)/shard_map/all_to_all | solution.py:70
  217.0 34.4 %all-to-all-start.1 = ((bf16[32,4,3584]{2,1,0:T(4,128)(2,1)}), bf16[32,4,3584]{2,1,0:T(4,128)(2,1)}, u32[]{:S(2)}, u32[]{:S(2)}) async-start(bf16[32,4,3584]{2,1,0:T(4,128)(2,1)} %reshape.528), calls=%async_computation.1 | async-start | bytes 1835008 | tf_op jit(solution)/shard_map/all_to_all | solution.py:70
  231.5 23.3 %copy-start.5 = (bf16[1,64,3584]{2,1,0:T(8,128)(2,1)S(1)}, bf16[1,64,3584]{2,1,0:T(8,128)(2,1)}, u32[]{:S(2)}) copy-start(bf16[1,64,3584]{2,1,0:T(8,128)(2,1)} %param.9) | copy-start | bytes 1376260
  231.5 28.8 %collective-permute-start.3 = (bf16[64,3584]{1,0:T(8,128)(2,1)}, bf16[64,3584]{1,0:T(8,128)(2,1)}, u32[]{:S(2)}, u32[]{:S(2)}) collective-permute-start(bf16[64,3584]{1,0:T(8,128)(2,1)} %fusion.3), channel_id=1, source_target_pairs={{32,0},{64,32},{96,64},{128,96},{160,128},{192,160},{224,192},{256... | collective-permute-start | bytes 1376264 | tf_op jit(solution)/shard_map/ppermute | solution.py:18
  254.8 8.8 %copy-start.11 = (s32[64,8]{0,1:T(8,128)S(1)}, s32[64,8]{0,1:T(8,128)}, u32[]{:S(2)}) copy-start(s32[64,8]{0,1:T(8,128)} %copy.66) | copy-start | bytes 6148
  257.2 14.2 %collective-permute-start = (bf16[64,3584]{1,0:T(8,128)(2,1)}, bf16[64,3584]{1,0:T(8,128)(2,1)S(1)}, u32[]{:S(2)}, u32[]{:S(2)}) collective-permute-start(bf16[64,3584]{1,0:T(8,128)(2,1)} %fusion), channel_id=1, source_target_pairs={{480,0},{0,32},{32,64},{64,96},{96,128},{128,160},{160,192},{192,2... | collective-permute-start | bytes 1376264 | tf_op jit(solution)/shard_map/ppermute | solution.py:18
  264.2 7.0 %copy-start.9 = (s32[1,4,4,128]{3,2,1,0:T(4,128)S(1)}, s32[1,4,4,128]{3,2,1,0:T(4,128)}, u32[]{:S(2)}) copy-start(s32[1,4,4,128]{3,2,1,0:T(4,128)} %add_bitcast_fusion.4) | copy-start | bytes 24580
  264.2 7.0 %copy-start.15 = (s32[512]{0:T(512)S(1)}, s32[512]{0:T(512)}, u32[]{:S(2)}) copy-start(s32[512]{0:T(512)} %eq.320) | copy-start | bytes 6148
  266.7 34.4 %all-to-all-start.8 = ((bf16[32,4,3584]{2,1,0:T(4,128)(2,1)}), bf16[32,4,3584]{2,1,0:T(4,128)(2,1)}, u32[]{:S(2)}, u32[]{:S(2)}) async-start(bf16[32,4,3584]{2,1,0:T(4,128)(2,1)} %bitcast.279), calls=%async_computation.8 | async-start | bytes 1835008 | tf_op jit(solution)/shard_map/all_to_all | solution.py:65
  302.3 34.4 %all-to-all-start.2 = ((bf16[32,4,3584]{2,1,0:T(4,128)(2,1)}), bf16[32,4,3584]{2,1,0:T(4,128)(2,1)}, u32[]{:S(2)}, u32[]{:S(2)}) async-start(bf16[32,4,3584]{2,1,0:T(4,128)(2,1)} %bitcast.282), calls=%async_computation.2 | async-start | bytes 1835008 | tf_op jit(solution)/shard_map/all_to_all | solution.py:65
  314.1 27.1 %copy-start.13 = (s32[1,1,64,8]{2,3,1,0:T(8,128)S(1)}, s32[1,1,64,8]{2,3,1,0:T(8,128)}, u32[]{:S(2)}) copy-start(s32[1,1,64,8]{2,3,1,0:T(8,128)} %get-tuple-element.16) | copy-start | bytes 6148
  336.8 34.4 %all-to-all-start.9 = ((bf16[32,4,3584]{2,1,0:T(4,128)(2,1)}), bf16[32,4,3584]{2,1,0:T(4,128)(2,1)}, u32[]{:S(2)}, u32[]{:S(2)}) async-start(bf16[32,4,3584]{2,1,0:T(4,128)(2,1)} %reshape.560), calls=%async_computation.9 | async-start | bytes 1835008 | tf_op jit(solution)/shard_map/all_to_all | solution.py:70
  348.7 29.0 %copy-start.12 = (s32[1,1,64,8]{2,3,1,0:T(8,128)S(1)}, s32[1,1,64,8]{2,3,1,0:T(8,128)}, u32[]{:S(2)}) copy-start(s32[1,1,64,8]{2,3,1,0:T(8,128)} %get-tuple-element.19) | copy-start | bytes 6148
  371.2 34.6 %all-to-all-start.3 = ((bf16[32,4,3584]{2,1,0:T(4,128)(2,1)}), bf16[32,4,3584]{2,1,0:T(4,128)(2,1)}, u32[]{:S(2)}, u32[]{:S(2)}) async-start(bf16[32,4,3584]{2,1,0:T(4,128)(2,1)} %reshape.536), calls=%async_computation.3 | async-start | bytes 1835008 | tf_op jit(solution)/shard_map/all_to_all | solution.py:70
  386.3 37.5 %collective-permute-start.4 = (bf16[64,3584]{1,0:T(8,128)(2,1)}, bf16[64,3584]{1,0:T(8,128)(2,1)}, u32[]{:S(2)}, u32[]{:S(2)}) collective-permute-start(bf16[64,3584]{1,0:T(8,128)(2,1)} %fusion.4), channel_id=1, source_target_pairs={{32,0},{64,32},{96,64},{128,96},{160,128},{192,160},{224,192},{256... | collective-permute-start | bytes 1376264 | tf_op jit(solution)/shard_map/ppermute | solution.py:18
  409.2 17.9 %copy-start.10 = (s32[64,8]{0,1:T(8,128)S(1)}, s32[64,8]{0,1:T(8,128)}, u32[]{:S(2)}) copy-start(s32[64,8]{0,1:T(8,128)} %copy.69) | copy-start | bytes 6148
  411.6 22.7 %collective-permute-start.1 = (bf16[64,3584]{1,0:T(8,128)(2,1)}, bf16[64,3584]{1,0:T(8,128)(2,1)S(1)}, u32[]{:S(2)}, u32[]{:S(2)}) collective-permute-start(bf16[64,3584]{1,0:T(8,128)(2,1)} %fusion.1), channel_id=1, source_target_pairs={{480,0},{0,32},{32,64},{64,96},{96,128},{128,160},{160,192},{192,2... | collective-permute-start | bytes 1376264 | tf_op jit(solution)/shard_map/ppermute | solution.py:18
  427.1 7.0 %copy-start.8 = (s32[1,4,4,128]{3,2,1,0:T(4,128)S(1)}, s32[1,4,4,128]{3,2,1,0:T(4,128)}, u32[]{:S(2)}) copy-start(s32[1,4,4,128]{3,2,1,0:T(4,128)} %add_bitcast_fusion.3) | copy-start | bytes 24580
  427.1 7.0 %copy-start.14 = (s32[512]{0:T(512)S(1)}, s32[512]{0:T(512)}, u32[]{:S(2)}) copy-start(s32[512]{0:T(512)} %eq.334) | copy-start | bytes 6148
  429.7 34.5 %all-to-all-start.10 = ((bf16[32,4,3584]{2,1,0:T(4,128)(2,1)}), bf16[32,4,3584]{2,1,0:T(4,128)(2,1)}, u32[]{:S(2)}, u32[]{:S(2)}) async-start(bf16[32,4,3584]{2,1,0:T(4,128)(2,1)} %bitcast.278), calls=%async_computation.10 | async-start | bytes 1835008 | tf_op jit(solution)/shard_map/all_to_all | solution.py:65
  465.4 7.1 %copy-start.3 = (bf16[1,3584,128]{2,1,0:T(8,128)(2,1)S(1)}, bf16[1,3584,128]{2,1,0:T(8,128)(2,1)}, u32[]{:S(2)}) copy-start(bf16[1,3584,128]{2,1,0:T(8,128)(2,1)} %param.15) | copy-start | bytes 2752516
  465.4 34.7 %all-to-all-start.4 = ((bf16[32,4,3584]{2,1,0:T(4,128)(2,1)}), bf16[32,4,3584]{2,1,0:T(4,128)(2,1)}, u32[]{:S(2)}, u32[]{:S(2)}) async-start(bf16[32,4,3584]{2,1,0:T(4,128)(2,1)} %bitcast.16), calls=%async_computation.4 | async-start | bytes 1835008 | tf_op jit(solution)/shard_map/all_to_all | solution.py:65
  500.1 34.5 %all-to-all-start.11 = ((bf16[32,4,3584]{2,1,0:T(4,128)(2,1)}), bf16[32,4,3584]{2,1,0:T(4,128)(2,1)}, u32[]{:S(2)}, u32[]{:S(2)}) async-start(bf16[32,4,3584]{2,1,0:T(4,128)(2,1)} %reshape.568), calls=%async_computation.11 | async-start | bytes 1835008 | tf_op jit(solution)/shard_map/all_to_all | solution.py:70
  534.6 33.8 %all-to-all-start.5 = ((bf16[32,4,3584]{2,1,0:T(4,128)(2,1)}), bf16[32,4,3584]{2,1,0:T(4,128)(2,1)S(1)}, u32[]{:S(2)}, u32[]{:S(2)}) async-start(bf16[32,4,3584]{2,1,0:T(4,128)(2,1)} %reshape.544), calls=%async_computation.5 | async-start | bytes 1835008 | tf_op jit(solution)/shard_map/all_to_all | solution.py:70
  543.0 28.8 %collective-permute-start.5 = (bf16[64,3584]{1,0:T(8,128)(2,1)}, bf16[64,3584]{1,0:T(8,128)(2,1)S(1)}, u32[]{:S(2)}, u32[]{:S(2)}) collective-permute-start(bf16[64,3584]{1,0:T(8,128)(2,1)} %fusion.5), channel_id=1, source_target_pairs={{32,0},{64,32},{96,64},{128,96},{160,128},{192,160},{224,192},{256... | collective-permute-start | bytes 1376264 | tf_op jit(solution)/shard_map/ppermute | solution.py:18
  569.8 13.6 %collective-permute-start.2 = (bf16[64,3584]{1,0:T(8,128)(2,1)S(1)}, bf16[64,3584]{1,0:T(8,128)(2,1)S(1)}, u32[]{:S(2)}, u32[]{:S(2)}) collective-permute-start(bf16[64,3584]{1,0:T(8,128)(2,1)S(1)} %fusion.2), channel_id=1, source_target_pairs={{480,0},{0,32},{32,64},{64,96},{96,128},{128,160},{160,192},{192,2... | collective-permute-start | bytes 1376264 | tf_op jit(solution)/shard_map/ppermute | solution.py:18
  (3 other events, 6.1 us)
Sparse Core Ops, SparseCore 0:
  11.4 92.7 all-gather.2
where the time goes:
time: 604 us; the launch traced here: 592 us
  waiting for transfers between devices  356 us (59%)
  starting transfers between devices  80.9 us (13%)
  matrix products  54.9 us (9%)
  local copies, waits for them, and re-layouts  50.5 us (8%)
  other arithmetic  34.4 us (6%)
  between operations  15.3 us (3%)
    all_to_all x6, waiting for transfers between devices, send_rows(): lax.all_to_all(copies[0], 'ep', split_axis=0, concat_axis=0, tiled=True)  141 us
    all_to_all x6, waiting for transfers between devices, return_rows(): lax.all_to_all(partials[0], 'ep', split_axis=0, concat_axis=0, tiled=True)  115 us
    all_gather x1, waiting for transfers between devices, body(): router_all = lax.all_gather(router[0], 'ep', axis=0, tiled=True)  87.5 us
    all_to_all x6, starting transfers between devices, send_rows(): lax.all_to_all(copies[0], 'ep', split_axis=0, concat_axis=0, tiled=True)  29.9 us
    all_to_all x6, starting transfers between devices, return_rows(): lax.all_to_all(partials[0], 'ep', split_axis=0, concat_axis=0, tiled=True)  26.3 us
    ppermute x6, starting transfers between devices, shifted(): return lax.ppermute(block, axis, route)  24.7 us
    dot_general x6, matrix products, expert_apply(): jnp.dot(hidden, w_down, preferred_element_type=jnp.float32)  17.2 us
    reshape x6, local copies, waits for them, and re-layouts, expert_apply(): flat_rows = token_rows.reshape(-1, row_shape[-1])  14.4 us
  transfers between devices with their start and end apart: 19, of which 14 were waited for; matrix products, arithmetic and copies ran while one was open for 22% of the time, Pallas kernels for 0%

commit v1 on v0

v1 whole, which is shorter than its diff:
```python
import jax
import jax.numpy as jnp
from jax import lax
from jax.experimental import pallas as pl
from jax.experimental.pallas import tpu as pltpu
from jax.sharding import PartitionSpec as P

MESH = pl.DeviceIdType.MESH
F32 = jnp.float32
BF16 = jnp.bfloat16

STEPS = 3
TOP = 8
CAP = 4
N_PP = 16
N_Y = 8
N_Q = 4
TOKS = 64
D = 3584
QW = D // N_Q
ROWS = N_Q * TOKS
UNIT = N_Q * CAP
HID = 128
EXPERTS = 256
HALF = D // 2

route_scale = 2.5
norm_eps = 1e-06


def iota(shape, dim):
    return lax.broadcasted_iota(jnp.int32, shape, dim)


def dot(a, b):
    return jnp.dot(a, b, preferred_element_type=F32)


def dot_t(a, b):
    return lax.dot_general(a, b, (((1,), (1,)), ((), ())), preferred_element_type=F32)


def one_hot(condition):
    return jnp.where(condition, 1.0, 0.0).astype(BF16)


def kernel(
    xr_in, xf_in, idr_in, idf_in, gain, router, wg_in, wu_in, wd_in,
    outr, outf,
    x, ids, normed, packed, zr, rrecv, osend, frecv, ssend, srecv, gsend, grecv,
    ubuf, obuf, acc, wgu, wd, perm, perm_t, rown, rgath, rall,
    sem_in, sem_w, ws_s, ws_r, rt_s, rt_r,
    ya_s, ya_r, yb_s, yb_r, ret_s, ret_r, z_s, z_r, x_s, x_r, s_s, s_r, g_s, g_r,
):
    pp, ep = lax.axis_index("pp"), lax.axis_index("ep")
    zh, y, c = ep // 16, (ep // 2) % N_Y, ep % 2
    oz = 1 - zh

    def at(rank, z, row, core):
        return {"pp": rank, "ep": z * 16 + row * 2 + core}

    def copy(src, dst, send, recv, to):
        return pltpu.make_async_remote_copy(
            src_ref=src, dst_ref=dst, send_sem=send, recv_sem=recv, device_id=to, device_id_type=MESH
        )

    def row_at(shift):
        return lax.rem(y + shift, N_Y)

    def next_rank(d):
        return lax.rem(pp + 1 - 2 * d + N_PP, N_PP)

    def weight_copies():
        low, high = pl.ds(0, HID), pl.ds(HID, HID)
        to = at(pp, zh, y, 1 - c)
        local = [
            pltpu.make_async_copy(wg_in.at[0], wgu.at[:, pl.ds(0, HID)], sem_w.at[0]),
            pltpu.make_async_copy(wu_in.at[0], wgu.at[:, pl.ds(2 * HID, HID)], sem_w.at[1]),
            pltpu.make_async_copy(wd_in.at[0], wd.at[low], sem_w.at[2]),
        ]
        remote = [
            copy(wg_in.at[0], wgu.at[:, pl.ds(HID, HID)], ws_s.at[0], ws_r.at[0], to),
            copy(wu_in.at[0], wgu.at[:, pl.ds(3 * HID, HID)], ws_s.at[1], ws_r.at[1], to),
            copy(wd_in.at[0], wd.at[high], ws_s.at[2], ws_r.at[2], to),
        ]
        return local, remote

    def router_z():
        return copy(rown, rgath.at[0, y, 1], rt_s.at[0], rt_r.at[0], at(pp, oz, y, c))

    def router_right(k):
        block = rgath.at[0, row_at(N_Y - k)]
        return copy(block, block, rt_s.at[1 + k], rt_r.at[1 + k], at(pp, zh, row_at(1), c))

    def router_left(k):
        block = rgath.at[0, row_at(k)]
        return copy(block, block, rt_s.at[5 + k], rt_r.at[5 + k], at(pp, zh, row_at(N_Y - 1), c))

    def router_core():
        return copy(rgath.at[0], rgath.at[1], rt_s.at[8], rt_r.at[8], at(pp, zh, y, 1 - c))

    def send_z(k):
        return copy(packed.at[k, pl.ds(2 * oz, 2)], zr.at[k], z_s.at[k], z_r.at[k], at(pp, oz, y, c))

    def send_ya(k, shift):
        row = row_at(shift)
        return copy(
            packed.at[k, 2 * zh + row // 4], rrecv.at[k, y, 0],
            ya_s.at[k, shift - 1], ya_r.at[k, shift - 1], at(pp, zh, row, c),
        )

    def send_yb(k, shift):
        row = row_at(shift)
        return copy(
            zr.at[k, row // 4], rrecv.at[k, y, 1],
            yb_s.at[k, shift - 1], yb_r.at[k, shift - 1], at(pp, zh, row, c),
        )

    def send_back(k, shift):
        row = row_at(shift)
        return copy(
            osend.at[k, row], frecv.at[k, y],
            ret_s.at[k, shift - 1], ret_r.at[k, shift - 1], at(pp, zh, row, c),
        )

    def send_x(k, d):
        return copy(x.at[k], x.at[k + 2], x_s.at[k], x_r.at[k], at(next_rank(d), zh, y, c))

    def send_sums(k, d):
        dst = srecv.at[k + 2, pl.ds(2 * zh, 2)]
        return [
            copy(ssend.at[k, 0], dst, s_s.at[k, 0], s_r.at[k, 0], at(next_rank(d), zh, y, c)),
            copy(ssend.at[k, 1], dst, s_s.at[k, 1], s_r.at[k, 1], at(next_rank(d), oz, y, c)),
        ]

    def send_gates(k, d):
        return copy(gsend.at[k], grecv.at[k + 2], g_s.at[k], g_r.at[k], at(next_rank(d), zh, y, c))

    def state_in(source, d):
        return [
            pltpu.make_async_copy(
                source.at[0, :, pl.ds(q * QW, QW)], x.at[d, pl.ds(q * TOKS, TOKS)], sem_in.at[d, q]
            )
            for q in range(N_Q)
        ]

    def state_out(d, target):
        return [
            pltpu.make_async_copy(
                x.at[2 * STEPS + d, pl.ds(q * TOKS, TOKS)], target.at[0, :, pl.ds(q * QW, QW)], sem_in.at[d, q]
            )
            for q in range(N_Q)
        ]

    loads = state_in(xr_in, 0) + state_in(xf_in, 1)
    for load in loads:
        load.start()
    local, remote = weight_copies()
    for w in local:
        w.start()
    barrier = pltpu.get_barrier_semaphore()
    peers = [at(pp, zh, row_at(shift), c) for shift in range(1, N_Y)]
    peers += [at(pp, oz, y, c), at(pp, zh, y, 1 - c)]
    for rank in (next_rank(0), next_rank(1)):
        peers += [at(rank, zh, y, c), at(rank, oz, y, c)]
    for peer in peers:
        pl.semaphore_signal(barrier, inc=1, device_id=peer, device_id_type=MESH)

    for s in range(STEPS):
        ids[2 * s] = idr_in[s, 0]
        ids[2 * s + 1] = idf_in[s, 0]
    for d in range(2):
        srecv[d] = jnp.zeros(srecv.shape[1:], BF16)
        grecv[d] = jnp.zeros(grecv.shape[1:], BF16)
    u, r = iota((ROWS, ROWS), 0), iota((ROWS, ROWS), 1)
    perm[...] = one_hot(
        ((u % 64) // 4 == r // 16) & (u // 64 == (r // 4) % 4) & (u % 4 == r % 4)
    )
    perm_t[...] = one_hot(
        ((r % 64) // 4 == u // 16) & (r // 64 == (u // 4) % 4) & (r % 4 == u % 4)
    )
    own = router[0].astype(F32)
    own = jnp.concatenate([own[:, :HALF], own[:, HALF:]], axis=0).astype(BF16)
    rown[...] = own
    rgath[0, y, 0] = own

    pl.semaphore_wait(barrier, len(peers))
    for w in remote:
        w.start()
    router_z().start()
    for load in loads:
        load.wait()

    lane = iota((TOKS, 128), 1)
    lane_e, lane_q, lane_c = (lane % 64) // UNIT, (lane // CAP) % N_Q, lane % CAP

    def matches(k):
        chosen = ids[k]
        hit = jnp.zeros((TOKS, 128), F32)
        for col in range(TOP):
            hit = hit + jnp.where(chosen[:, col : col + 1] == lane_e, 1.0, 0.0)
        before = one_hot(iota((TOKS, TOKS), 0) > iota((TOKS, TOKS), 1))
        earlier = dot(before, hit.astype(BF16))
        return jnp.where(earlier == lane_c.astype(F32), hit, 0.0)

    def by_quarter(table):
        return jnp.concatenate([jnp.where(lane_q == q, table, 0.0) for q in range(N_Q)], axis=0)

    def receive_state(k):
        gates = by_quarter(grecv[k].astype(F32)).astype(BF16)
        sums = srecv[k].reshape(4 * UNIT, QW)
        acc[...] = dot(gates, jnp.concatenate([sums, sums], axis=0))
        squares = jnp.zeros((TOKS, 1), F32)
        for q in range(N_Q):
            rows = pl.ds(q * TOKS, TOKS)
            now = (x[k, rows].astype(F32) + acc[rows]).astype(BF16)
            x[k, rows] = now
            now = now.astype(F32)
            squares = squares + jnp.sum(now * now, axis=-1, keepdims=True)
        return squares

    def wait_state(k, d):
        send_x(k - 2, d).wait_recv()
        for sums in send_sums(k - 2, d):
            sums.wait_recv()
        send_gates(k - 2, d).wait_recv()

    def dispatch(s, d):
        k = 2 * s + d

        @pl.when(s > 0)
        def _():
            wait_state(k, d)

        squares = receive_state(k)
        inverse = lax.rsqrt(squares * (1.0 / D) + norm_eps)
        for q in range(N_Q):
            rows = pl.ds(q * TOKS, TOKS)
            scaled = x[k, rows].astype(F32) * inverse * gain[:, pl.ds(q * QW, QW)]
            normed[d, rows] = scaled.astype(BF16)
        pick = by_quarter(matches(k)).T[: 4 * UNIT].astype(BF16)
        packed[k] = dot(pick, normed[d]).astype(BF16).reshape(4, UNIT, QW)
        send_z(k).start()
        for shift in range(1, N_Y):
            send_ya(k, shift).start()
        send_x(k, d).start()
        rrecv[k, y, 0] = packed[k, 2 * zh + y // 4]

    def relay(s, d):
        k = 2 * s + d
        send_z(k).wait_recv()
        for shift in range(1, N_Y):
            send_yb(k, shift).start()
        rrecv[k, y, 1] = zr[k, y // 4]

    def gather_router():
        router_z().wait_recv()
        for k in range(4):
            if k:
                router_right(k - 1).wait_recv()
            router_right(k).start()
            if k < 3:
                if k:
                    router_left(k - 1).wait_recv()
                router_left(k).start()
        router_left(2).wait_recv()
        router_right(3).wait_recv()
        router_core().start()
        router_core().wait_recv()
        blocks = rgath[...].reshape(2 * EXPERTS, HALF)
        n, row = iota((EXPERTS, 2 * EXPERTS), 0), iota((EXPERTS, 2 * EXPERTS), 1)
        core, place = (row // 256 + c) % 2, (row // 32) % 8
        z = ((row // 16) % 2 + zh) % 2
        expert = (z * 16 + place * 2 + core) * 8 + row % 8
        for h in range(2):
            pick = one_hot((expert == n) & ((row // 8) % 2 == h))
            for part in range(2):
                cols = pl.ds(part * QW, QW)
                rall[2 * h + part] = dot(pick, rgath[:, :, :, :, cols].reshape(2 * EXPERTS, QW)).astype(BF16)

    def gate_table(s, d):
        k = 2 * s + d
        logits = jnp.zeros((TOKS, EXPERTS), F32)
        for q in range(N_Q):
            logits = logits + dot_t(normed[d, pl.ds(q * TOKS, TOKS)], rall[q])
        affinity = jax.nn.sigmoid(logits)
        chosen = ids[k]
        column = iota((TOKS, EXPERTS), 1)
        named = jnp.zeros((TOKS, EXPERTS), F32)
        for col in range(TOP):
            named = named + jnp.where(chosen[:, col : col + 1] == column, affinity, 0.0)
        total = jnp.sum(named, axis=-1, keepdims=True)
        weights = route_scale * affinity[:, :4] / total
        table = jnp.zeros((TOKS, 128), F32)
        for e in range(4):
            table = jnp.where(lane_e == e, weights[:, e : e + 1], table)
        table = table * matches(k)
        high = table.astype(BF16)
        low = (table - high.astype(F32)).astype(BF16)
        gsend[k] = jnp.where(lane < 64, high.astype(F32), low.astype(F32)).astype(BF16)
        send_gates(k, d).start()

    def experts(s, d):
        k = 2 * s + d
        for shift in range(1, N_Y):
            send_ya(k, shift).wait_recv()
        for shift in range(1, N_Y):
            send_yb(k, shift).wait_recv()
        ubuf[...] = dot(perm[...], rrecv[k].reshape(ROWS, QW)).astype(BF16)
        both = jnp.zeros((TOKS, 4 * HID), F32)
        for q in range(N_Q):
            both = both + dot(ubuf[pl.ds(q * TOKS, TOKS)], wgu[pl.ds(q * QW, QW)])
        gate, up = both[:, : 2 * HID], both[:, 2 * HID :]
        hidden = (gate * jax.nn.sigmoid(gate) * up).astype(BF16)
        for q in range(N_Q):
            obuf[pl.ds(q * TOKS, TOKS)] = dot(hidden, wd[:, pl.ds(q * QW, QW)]).astype(BF16)
        osend[k] = dot(perm_t[...], obuf[...]).astype(BF16).reshape(N_Y, 2, UNIT, QW)
        for shift in range(1, N_Y):
            send_back(k, shift).start()
        frecv[k, y] = osend[k, y]

    def finish(s, d):
        k = 2 * s + d
        for shift in range(1, N_Y):
            send_back(k, shift).wait_recv()
        for zs in range(2):
            for e in range(2):
                total = frecv[k, 4 * e, zs].astype(F32)
                for i in range(1, 4):
                    total = total + frecv[k, 4 * e + i, zs].astype(F32)
                ssend[k, zs, e] = total.astype(BF16)
        for sums in send_sums(k, d):
            sums.start()

    def both(phase, s):
        def one(d, carry):
            phase(s, d)
            return carry

        lax.fori_loop(0, 2, one, 0)

    def step(s, carry):
        both(dispatch, s)
        both(relay, s)

        @pl.when(s == 0)
        def _():
            gather_router()

        both(gate_table, s)

        @pl.when(s == 0)
        def _():
            for w in local:
                w.wait()
            for w in remote:
                w.wait_recv()

        both(experts, s)
        both(finish, s)
        return carry

    lax.fori_loop(0, STEPS, step, 0)

    def last(d, carry):
        k = 2 * STEPS + d
        wait_state(k, d)
        receive_state(k)
        return carry

    lax.fori_loop(0, 2, last, 0)
    stores = state_out(0, outr) + state_out(1, outf)
    for store in stores:
        store.start()

    for w in remote:
        w.wait_send()
    router_z().wait_send()
    for k in range(4):
        router_right(k).wait_send()
    for k in range(3):
        router_left(k).wait_send()
    router_core().wait_send()

    def drain(k, carry):
        d = lax.rem(k, 2)
        send_z(k).wait_send()
        for shift in range(1, N_Y):
            send_ya(k, shift).wait_send()
            send_yb(k, shift).wait_send()
            send_back(k, shift).wait_send()
        send_x(k, d).wait_send()
        for sums in send_sums(k, d):
            sums.wait_send()
        send_gates(k, d).wait_send()
        return carry

    lax.fori_loop(0, 2 * STEPS, drain, 0)
    for store in stores:
        store.wait()


def body(rising, falling, rising_ids, falling_ids, norm_gain, router, w_gate, w_up, w_down):
    K = 2 * STEPS
    dma = pltpu.SemaphoreType.DMA
    any_space, vmem = pl.BlockSpec(memory_space=pl.ANY), pl.BlockSpec(memory_space=pltpu.VMEM)
    buffers = [
        ((K + 2, ROWS, QW), BF16),
        ((K, TOKS, TOP), jnp.int32),
        ((2, ROWS, QW), BF16),
        ((K, 4, UNIT, QW), BF16),
        ((K, 2, UNIT, QW), BF16),
        ((K, N_Y, 2, UNIT, QW), BF16),
        ((K, N_Y, 2, UNIT, QW), BF16),
        ((K, N_Y, 2, UNIT, QW), BF16),
        ((K, 2, 2, UNIT, QW), BF16),
        ((K + 2, 4, UNIT, QW), BF16),
        ((K, TOKS, 128), BF16),
        ((K + 2, TOKS, 128), BF16),
        ((ROWS, QW), BF16),
        ((ROWS, QW), BF16),
        ((ROWS, QW), F32),
        ((D, 4 * HID), BF16),
        ((2 * HID, D), BF16),
        ((ROWS, ROWS), BF16),
        ((ROWS, ROWS), BF16),
        ((16, HALF), BF16),
        ((2, N_Y, 2, 16, HALF), BF16),
        ((N_Q, EXPERTS, QW), BF16),
    ]
    semaphores = [
        (2, N_Q), (3,), (3,), (3,), (9,), (9,),
        (K, 7), (K, 7), (K, 7), (K, 7), (K, 7), (K, 7),
        (K,), (K,), (K,), (K,), (K, 2), (K, 2), (K,), (K,),
    ]
    return pl.pallas_call(
        kernel,
        out_shape=[jax.ShapeDtypeStruct(rising.shape, BF16)] * 2,
        in_specs=[any_space, any_space, vmem, vmem, vmem, vmem, any_space, any_space, any_space],
        out_specs=[any_space, any_space],
        scratch_shapes=[pltpu.VMEM(shape, dtype) for shape, dtype in buffers] + [dma(shape) for shape in semaphores],
        compiler_params=pltpu.CompilerParams(
            collective_id=0, has_side_effects=True, vmem_limit_bytes=56 * 1024 * 1024
        ),
        name="moe_relay",
    )(rising, falling, rising_ids, falling_ids, norm_gain, router, w_gate, w_up, w_down)


def solution(mesh):
    return jax.shard_map(
        body,
        mesh=mesh,
        in_specs=(
            P("pp", "ep", None),
            P("pp", "ep", None),
            P(None, "pp", "ep", None),
            P(None, "pp", "ep", None),
            P("pp", None),
            P("pp", "ep", None),
            P("pp", None, "ep"),
            P("pp", None, "ep"),
            P("pp", "ep", None),
        ),
        out_specs=(P("pp", "ep", None), P("pp", "ep", None)),
        check_vma=False,
    )
```

time: 604 us -> 197 us (0.33)
  the two profiles are of different devices: /device:TPU:76 before, /device:TPU:68 now
where the time goes in v1:
time: 197 us
  Pallas kernels  191 us (97%)
  local copies, waits for them, and re-layouts  4.84 us (2%)
    pallas_call x1, Pallas kernels, body(): pl.pallas_call(kernel, out_shape=[jax.ShapeDtypeStruct(rising.shape, BF16...  191 us
    unnamed x8, local copies, waits for them, and re-layouts  4.84 us

profile of v1, /device:TPU:68, one launch (start us, length us, event | category | flops | bytes accessed | tf_op | source)
XLA Modules:
  0.0 196.9 jit_solution(5475233697889277066)
XLA Ops:
  0.6 0.0 copy-start.1
  0.6 1.5 copy.11.idr_in
  2.1 0.0 copy-done.1
  2.1 0.7 copy.12.idf_in
  2.8 191.4 %moe_relay.1 = (bf16[1,64,3584]{2,1,0:T(8,128)(2,1)}, bf16[1,64,3584]{2,1,0:T(8,128)(2,1)}) custom-call(bf16[1,64,3584]{2,1,0:T(8,128)(2,1)} %xr_in.1, bf16[1,64,3584]{2,1,0:T(8,128)(2,1)} %xf_in.1, s32[3,1,64,8]{3,2,1,0:T(8,128)} %copy.11.idr_in, s32[3,1,64,8]{3,2,1,0:T(8,128)} %copy.12.idf_in, f32[1,3584]{1,0:T(1,128)} %gain.1, ...), custom_call_target="tpu_custom_call" | custom-call | tf_op jit(solution)/shard_map/moe_relay/pallas_call | solution.py:436
  194.2 0.0 copy-start
  194.2 1.9 copy.15
  196.1 0.0 copy-done
  196.1 0.8 copy.16
Async XLA Ops:
  0.6 1.5 copy-start.1
  194.2 1.9 copy-start

commit v2 on v1

--- a/solution.py
+++ b/solution.py
@@ -225,14 +225,12 @@
             sums.wait_recv()
         send_gates(k - 2, d).wait_recv()
 
-    def dispatch(s, d):
-        k = 2 * s + d
-
-        @pl.when(s > 0)
-        def _():
-            wait_state(k, d)
-
-        squares = receive_state(k)
+    def at_start(s, more, action):
+        @pl.when((s == 0) & more)
+        def _():
+            action()
+
+    def dispatch(k, s, d, squares):
         inverse = lax.rsqrt(squares * (1.0 / D) + norm_eps)
         for q in range(N_Q):
             rows = pl.ds(q * TOKS, TOKS)
@@ -240,6 +238,7 @@
             normed[d, rows] = scaled.astype(BF16)
         pick = by_quarter(matches(k)).T[: 4 * UNIT].astype(BF16)
         packed[k] = dot(pick, normed[d]).astype(BF16).reshape(4, UNIT, QW)
+        at_start(s, d == 0, lambda: router_hop(0))
         send_z(k).start()
         for shift in range(1, N_Y):
             send_ya(k, shift).start()
@@ -253,21 +252,20 @@
             send_yb(k, shift).start()
         rrecv[k, y, 1] = zr[k, y // 4]
 
-    def gather_router():
-        router_z().wait_recv()
-        for k in range(4):
-            if k:
-                router_right(k - 1).wait_recv()
+    def router_hop(k):
+        if k == 0:
+            router_z().wait_recv()
+        else:
+            router_right(k - 1).wait_recv()
+        if k < 4:
             router_right(k).start()
-            if k < 3:
-                if k:
-                    router_left(k - 1).wait_recv()
-                router_left(k).start()
-        router_left(2).wait_recv()
-        router_right(3).wait_recv()
-        router_core().start()
+        if 0 < k < 4:
+            router_left(k - 1).wait_recv()
+        if k < 3:
+            router_left(k).start()
+
+    def order_router():
         router_core().wait_recv()
-        blocks = rgath[...].reshape(2 * EXPERTS, HALF)
         n, row = iota((EXPERTS, 2 * EXPERTS), 0), iota((EXPERTS, 2 * EXPERTS), 1)
         core, place = (row // 256 + c) % 2, (row // 32) % 8
         z = ((row // 16) % 2 + zh) % 2
@@ -332,7 +330,48 @@
         for sums in send_sums(k, d):
             sums.start()
 
-    def both(phase, s):
+    def results(s, d):
+        k = 2 * s + d
+
+        @pl.when(s > 0)
+        def _():
+            finish(s - 1, d)
+
+        @pl.when((s > 0) & (d == 0))
+        def _():
+            gate_table(s - 1, 1)
+
+        @pl.when((s < STEPS) & (d == 1))
+        def _():
+            relay(s, 0)
+            at_start(s, True, lambda: router_hop(1))
+
+        @pl.when(s > 0)
+        def _():
+            wait_state(k, d)
+
+        squares = receive_state(k)
+
+        @pl.when(s < STEPS)
+        def _():
+            dispatch(k, s, d, squares)
+
+    def mlp(s, d):
+        at_start(s, d == 0, wait_weights)
+        experts(s, d)
+
+        @pl.when((s == 0) & (d == 0))
+        def _():
+            router_hop(4)
+            router_core().start()
+
+    def wait_weights():
+        for w in local:
+            w.wait()
+        for w in remote:
+            w.wait_recv()
+
+    def twice(phase, s):
         def one(d, carry):
             phase(s, d)
             return carry
@@ -340,35 +379,20 @@
         lax.fori_loop(0, 2, one, 0)
 
     def step(s, carry):
-        both(dispatch, s)
-        both(relay, s)
-
-        @pl.when(s == 0)
-        def _():
-            gather_router()
-
-        both(gate_table, s)
-
-        @pl.when(s == 0)
-        def _():
-            for w in local:
-                w.wait()
-            for w in remote:
-                w.wait_recv()
-
-        both(experts, s)
-        both(finish, s)
+        twice(results, s)
+
+        @pl.when(s < STEPS)
+        def _():
+            at_start(s, True, lambda: router_hop(2))
+            relay(s, 1)
+            at_start(s, True, lambda: router_hop(3))
+            twice(mlp, s)
+            at_start(s, True, order_router)
+            gate_table(s, 0)
+
         return carry
 
-    lax.fori_loop(0, STEPS, step, 0)
-
-    def last(d, carry):
-        k = 2 * STEPS + d
-        wait_state(k, d)
-        receive_state(k)
-        return carry
-
-    lax.fori_loop(0, 2, last, 0)
+    lax.fori_loop(0, STEPS + 1, step, 0)
     stores = state_out(0, outr) + state_out(1, outf)
     for store in stores:
         store.start()

time: 197 us -> 180 us (0.914)
  the two profiles are of different devices: /device:TPU:68 before, /device:TPU:128 now
where the time goes in v2:
time: 180 us
  Pallas kernels  175 us (97%)
  local copies, waits for them, and re-layouts  4.84 us (3%)
    pallas_call x1, Pallas kernels, body(): pl.pallas_call(kernel, out_shape=[jax.ShapeDtypeStruct(rising.shape, BF16...  175 us
    unnamed x8, local copies, waits for them, and re-layouts  4.84 us

profile of v2, /device:TPU:128, one launch (start us, length us, event | category | flops | bytes accessed | tf_op | source)
XLA Modules:
  0.0 180.2 jit_solution(5090313365390079686)
XLA Ops:
  0.6 0.0 copy-start.1
  0.6 1.5 copy.11.idr_in
  2.1 0.0 copy-done.1
  2.1 0.7 copy.12.idf_in
  2.8 174.7 %moe_relay.1 = (bf16[1,64,3584]{2,1,0:T(8,128)(2,1)}, bf16[1,64,3584]{2,1,0:T(8,128)(2,1)}) custom-call(bf16[1,64,3584]{2,1,0:T(8,128)(2,1)} %xr_in.1, bf16[1,64,3584]{2,1,0:T(8,128)(2,1)} %xf_in.1, s32[3,1,64,8]{3,2,1,0:T(8,128)} %copy.11.idr_in, s32[3,1,64,8]{3,2,1,0:T(8,128)} %copy.12.idf_in, f32[1,3584]{1,0:T(1,128)} %gain.1, ...), custom_call_target="tpu_custom_call" | custom-call | tf_op jit(solution)/shard_map/moe_relay/pallas_call | solution.py:460
  177.6 0.0 copy-start
  177.6 1.9 %copy.15 = bf16[1,64,3584]{2,1,0:T(8,128)(2,1)} copy(bf16[1,64,3584]{2,1,0:T(8,128)(2,1)} %get-tuple-element.4) | data formatting | bytes 917504
  179.5 0.0 copy-done
  179.5 0.8 copy.16
Async XLA Ops:
  0.6 1.5 copy-start.1
  177.6 1.9 %copy-start = (bf16[1,64,3584]{2,1,0:T(8,128)(2,1)S(1)}, bf16[1,64,3584]{2,1,0:T(8,128)(2,1)}, u32[]{:S(2)}) copy-start(bf16[1,64,3584]{2,1,0:T(8,128)(2,1)} %get-tuple-element.5) | copy-start | bytes 1376260

commit v3 on v2

--- a/solution.py
+++ b/solution.py
@@ -85,19 +85,22 @@
         ]
         return local, remote
 
+    def router_pair():
+        return copy(rown, rgath.at[y, 0, 0], rt_s.at[9], rt_r.at[9], at(pp, zh, y, 1))
+
     def router_z():
-        return copy(rown, rgath.at[0, y, 1], rt_s.at[0], rt_r.at[0], at(pp, oz, y, c))
+        return copy(rgath.at[y, 0], rgath.at[y, 1], rt_s.at[0], rt_r.at[0], at(pp, oz, y, 1))
 
     def router_right(k):
-        block = rgath.at[0, row_at(N_Y - k)]
-        return copy(block, block, rt_s.at[1 + k], rt_r.at[1 + k], at(pp, zh, row_at(1), c))
+        block = rgath.at[row_at(N_Y - k)]
+        return copy(block, block, rt_s.at[1 + k], rt_r.at[1 + k], at(pp, zh, row_at(1), 1))
 
     def router_left(k):
-        block = rgath.at[0, row_at(k)]
-        return copy(block, block, rt_s.at[5 + k], rt_r.at[5 + k], at(pp, zh, row_at(N_Y - 1), c))
+        block = rgath.at[row_at(k)]
+        return copy(block, block, rt_s.at[5 + k], rt_r.at[5 + k], at(pp, zh, row_at(N_Y - 1), 1))
 
     def router_core():
-        return copy(rgath.at[0], rgath.at[1], rt_s.at[8], rt_r.at[8], at(pp, zh, y, 1 - c))
+        return copy(rgath, rgath, rt_s.at[8], rt_r.at[8], at(pp, zh, y, 0))
 
     def send_z(k):
         return copy(packed.at[k, pl.ds(2 * oz, 2)], zr.at[k], z_s.at[k], z_r.at[k], at(pp, oz, y, c))
@@ -167,28 +170,17 @@
         pl.semaphore_signal(barrier, inc=1, device_id=peer, device_id_type=MESH)
 
     for s in range(STEPS):
-        ids[2 * s] = idr_in[s, 0]
-        ids[2 * s + 1] = idf_in[s, 0]
-    for d in range(2):
-        srecv[d] = jnp.zeros(srecv.shape[1:], BF16)
-        grecv[d] = jnp.zeros(grecv.shape[1:], BF16)
-    u, r = iota((ROWS, ROWS), 0), iota((ROWS, ROWS), 1)
-    perm[...] = one_hot(
-        ((u % 64) // 4 == r // 16) & (u // 64 == (r // 4) % 4) & (u % 4 == r % 4)
-    )
-    perm_t[...] = one_hot(
-        ((r % 64) // 4 == u // 16) & (r // 64 == (u // 4) % 4) & (r % 4 == u % 4)
-    )
+        ids[2 * s] = idr_in[s, 0].T
+        ids[2 * s + 1] = idf_in[s, 0].T
     own = router[0].astype(F32)
     own = jnp.concatenate([own[:, :HALF], own[:, HALF:]], axis=0).astype(BF16)
     rown[...] = own
-    rgath[0, y, 0] = own
-
-    pl.semaphore_wait(barrier, len(peers))
-    for w in remote:
-        w.start()
-    router_z().start()
-    for load in loads:
+
+    @pl.when(c == 1)
+    def _():
+        rgath[y, 0, 1] = own
+
+    for load in loads[:N_Q]:
         load.wait()
 
     lane = iota((TOKS, 128), 1)
@@ -219,6 +211,13 @@
             squares = squares + jnp.sum(now * now, axis=-1, keepdims=True)
         return squares
 
+    def first_state(d):
+        squares = jnp.zeros((TOKS, 1), F32)
+        for q in range(N_Q):
+            now = x[d, pl.ds(q * TOKS, TOKS)].astype(F32)
+            squares = squares + jnp.sum(now * now, axis=-1, keepdims=True)
+        return squares
+
     def wait_state(k, d):
         send_x(k - 2, d).wait_recv()
         for sums in send_sums(k - 2, d):
@@ -230,7 +229,30 @@
         def _():
             action()
 
-    def dispatch(k, s, d, squares):
+    def enter():
+        pl.semaphore_wait(barrier, len(peers))
+
+        @pl.when(c == 0)
+        def _():
+            router_pair().start()
+
+    def constants():
+        for w in remote:
+            w.start()
+        u, r = iota((ROWS, ROWS), 0), iota((ROWS, ROWS), 1)
+        perm[...] = one_hot(
+            ((u % 64) // 4 == r // 16) & (u // 64 == (r // 4) % 4) & (u % 4 == r % 4)
+        )
+        perm_t[...] = one_hot(
+            ((r % 64) // 4 == u // 16) & (r // 64 == (u // 4) % 4) & (r % 4 == u % 4)
+        )
+
+        @pl.when(c == 1)
+        def _():
+            router_pair().wait_recv()
+            router_z().start()
+
+    def dispatch(k, d, squares, first=False):
         inverse = lax.rsqrt(squares * (1.0 / D) + norm_eps)
         for q in range(N_Q):
             rows = pl.ds(q * TOKS, TOKS)
@@ -238,12 +260,14 @@
             normed[d, rows] = scaled.astype(BF16)
         pick = by_quarter(matches(k)).T[: 4 * UNIT].astype(BF16)
         packed[k] = dot(pick, normed[d]).astype(BF16).reshape(4, UNIT, QW)
-        at_start(s, d == 0, lambda: router_hop(0))
+        if first:
+            enter()
         send_z(k).start()
         for shift in range(1, N_Y):
             send_ya(k, shift).start()
-        send_x(k, d).start()
         rrecv[k, y, 0] = packed[k, 2 * zh + y // 4]
+        if first:
+            constants()
 
     def relay(s, d):
         k = 2 * s + d
@@ -253,22 +277,31 @@
         rrecv[k, y, 1] = zr[k, y // 4]
 
     def router_hop(k):
-        if k == 0:
-            router_z().wait_recv()
-        else:
-            router_right(k - 1).wait_recv()
-        if k < 4:
-            router_right(k).start()
-        if 0 < k < 4:
-            router_left(k - 1).wait_recv()
-        if k < 3:
-            router_left(k).start()
+        @pl.when(c == 1)
+        def _():
+            if k == 0:
+                router_z().wait_recv()
+            else:
+                router_right(k - 1).wait_recv()
+            if k < 4:
+                router_right(k).start()
+            if 0 < k < 4:
+                router_left(k - 1).wait_recv()
+            if k < 3:
+                router_left(k).start()
+            if k == 4:
+                router_core().start()
 
     def order_router():
-        router_core().wait_recv()
+        router_hop(4)
+
+        @pl.when(c == 0)
+        def _():
+            router_core().wait_recv()
+
         n, row = iota((EXPERTS, 2 * EXPERTS), 0), iota((EXPERTS, 2 * EXPERTS), 1)
-        core, place = (row // 256 + c) % 2, (row // 32) % 8
-        z = ((row // 16) % 2 + zh) % 2
+        core, place = (row // 16) % 2, row // 64
+        z = ((row // 32) % 2 + zh) % 2
         expert = (z * 16 + place * 2 + core) * 8 + row % 8
         for h in range(2):
             pick = one_hot((expert == n) & ((row // 8) % 2 == h))
@@ -331,39 +364,29 @@
             sums.start()
 
     def results(s, d):
-        k = 2 * s + d
-
-        @pl.when(s > 0)
-        def _():
-            finish(s - 1, d)
-
-        @pl.when((s > 0) & (d == 0))
-        def _():
-            gate_table(s - 1, 1)
-
-        @pl.when((s < STEPS) & (d == 1))
-        def _():
-            relay(s, 0)
-            at_start(s, True, lambda: router_hop(1))
-
-        @pl.when(s > 0)
-        def _():
-            wait_state(k, d)
-
+        k = 2 * s + 2 + d
+        finish(s, d)
+
+        @pl.when(d == 0)
+        def _():
+            gate_table(s, 1)
+
+        @pl.when((s < STEPS - 1) & (d == 1))
+        def _():
+            relay(s + 1, 0)
+
+        wait_state(k, d)
         squares = receive_state(k)
 
-        @pl.when(s < STEPS)
-        def _():
-            dispatch(k, s, d, squares)
+        @pl.when(s < STEPS - 1)
+        def _():
+            dispatch(k, d, squares)
 
     def mlp(s, d):
         at_start(s, d == 0, wait_weights)
         experts(s, d)
 
-        @pl.when((s == 0) & (d == 0))
-        def _():
-            router_hop(4)
-            router_core().start()
+        at_start(s, d == 0, lambda: router_hop(3))
 
     def wait_weights():
         for w in local:
@@ -379,32 +402,43 @@
         lax.fori_loop(0, 2, one, 0)
 
     def step(s, carry):
+        relay(s, 1)
+        send_x(2 * s, 0).start()
+        send_x(2 * s + 1, 1).start()
+        at_start(s, True, lambda: router_hop(2))
+        twice(mlp, s)
+        at_start(s, True, order_router)
+        gate_table(s, 0)
         twice(results, s)
-
-        @pl.when(s < STEPS)
-        def _():
-            at_start(s, True, lambda: router_hop(2))
-            relay(s, 1)
-            at_start(s, True, lambda: router_hop(3))
-            twice(mlp, s)
-            at_start(s, True, order_router)
-            gate_table(s, 0)
-
         return carry
 
-    lax.fori_loop(0, STEPS + 1, step, 0)
+    dispatch(0, 0, first_state(0), first=True)
+    router_hop(0)
+    relay(0, 0)
+    for load in loads[N_Q:]:
+        load.wait()
+    dispatch(1, 1, first_state(1))
+    router_hop(1)
+    lax.fori_loop(0, STEPS, step, 0)
     stores = state_out(0, outr) + state_out(1, outf)
     for store in stores:
         store.start()
 
     for w in remote:
         w.wait_send()
-    router_z().wait_send()
-    for k in range(4):
-        router_right(k).wait_send()
-    for k in range(3):
-        router_left(k).wait_send()
-    router_core().wait_send()
+
+    @pl.when(c == 0)
+    def _():
+        router_pair().wait_send()
+
+    @pl.when(c == 1)
+    def _():
+        router_z().wait_send()
+        for k in range(4):
+            router_right(k).wait_send()
+        for k in range(3):
+            router_left(k).wait_send()
+        router_core().wait_send()
 
     def drain(k, carry):
         d = lax.rem(k, 2)
@@ -449,11 +483,11 @@
         ((ROWS, ROWS), BF16),
         ((ROWS, ROWS), BF16),
         ((16, HALF), BF16),
-        ((2, N_Y, 2, 16, HALF), BF16),
+        ((N_Y, 2, 2, 16, HALF), BF16),
         ((N_Q, EXPERTS, QW), BF16),
     ]
     semaphores = [
-        (2, N_Q), (3,), (3,), (3,), (9,), (9,),
+        (2, N_Q), (3,), (3,), (3,), (10,), (10,),
         (K, 7), (K, 7), (K, 7), (K, 7), (K, 7), (K, 7),
         (K,), (K,), (K,), (K,), (K, 2), (K, 2), (K,), (K,),
     ]
@@ -467,7 +501,7 @@
             collective_id=0, has_side_effects=True, vmem_limit_bytes=56 * 1024 * 1024
         ),
         name="moe_relay",
-    )(rising, falling, rising_ids, falling_ids, norm_gain, router, w_gate, w_up, w_down)
+    )(rising, falling, jnp.swapaxes(rising_ids, 2, 3), jnp.swapaxes(falling_ids, 2, 3), norm_gain, router, w_gate, w_up, w_down)
 
 
 def solution(mesh):

time: 180 us -> 173 us (0.961)
  the two profiles are of different devices: /device:TPU:128 before, /device:TPU:2 now
where the time goes in v3:
time: 173 us; the launch traced here: 172 us
  Pallas kernels  169 us (98%)
  local copies, waits for them, and re-layouts  2.64 us (2%)
    pallas_call x1, Pallas kernels, body(): pl.pallas_call(kernel, out_shape=[jax.ShapeDtypeStruct(rising.shape, BF16...  169 us

profile of v3, /device:TPU:2, one launch (start us, length us, event | category | flops | bytes accessed | tf_op | source)
XLA Modules:
  0.0 172.5 jit_solution(9385771450326090677)
XLA Ops:
  0.6 169.2 %moe_relay.1 = (bf16[1,64,3584]{2,1,0:T(8,128)(2,1)}, bf16[1,64,3584]{2,1,0:T(8,128)(2,1)}) custom-call(bf16[1,64,3584]{2,1,0:T(8,128)(2,1)} %xr_in.1, bf16[1,64,3584]{2,1,0:T(8,128)(2,1)} %xf_in.1, s32[3,1,8,64]{3,2,1,0:T(8,128)} %bitcast.2, s32[3,1,8,64]{3,2,1,0:T(8,128)} %bitcast.3, f32[1,3584]{1,0:T(1,128)} %gain.1, bf16[1,8,3584]{2,1,0:T(8,128)(2,1)} %router.1, ...), custom_call_target="tpu_custom_call" | custom-call | tf_op jit(solution)/shard_map/moe_relay/pallas_call | solution.py:494
  169.8 0.0 copy-start
  169.8 1.9 %copy.13 = bf16[1,64,3584]{2,1,0:T(8,128)(2,1)} copy(bf16[1,64,3584]{2,1,0:T(8,128)(2,1)} %get-tuple-element.4) | data formatting | bytes 917504
  171.7 0.0 copy-done
  171.7 0.8 copy.14
Async XLA Ops:
  169.8 1.9 %copy-start = (bf16[1,64,3584]{2,1,0:T(8,128)(2,1)S(1)}, bf16[1,64,3584]{2,1,0:T(8,128)(2,1)}, u32[]{:S(2)}) copy-start(bf16[1,64,3584]{2,1,0:T(8,128)(2,1)} %get-tuple-element.5) | copy-start | bytes 1376260

commit v4 on v3

--- a/solution.py
+++ b/solution.py
@@ -47,14 +47,16 @@
 def kernel(
     xr_in, xf_in, idr_in, idf_in, gain, router, wg_in, wu_in, wd_in,
     outr, outf,
-    x, ids, normed, packed, zr, rrecv, osend, frecv, ssend, srecv, gsend, grecv,
+    x, ids, normed, packed, zr, rrecv, osend, half, rsend, frecv, ssend, srecv, gsend, grecv,
     ubuf, obuf, acc, wgu, wd, perm, perm_t, rown, rgath, rall,
     sem_in, sem_w, ws_s, ws_r, rt_s, rt_r,
-    ya_s, ya_r, yb_s, yb_r, ret_s, ret_r, z_s, z_r, x_s, x_r, s_s, s_r, g_s, g_r,
+    ya_s, ya_r, yb_s, yb_r, ret_s, ret_r, on_s, on_r, half_s, half_r, z_s, z_r, x_s, x_r, s_s, s_r, g_s, g_r,
 ):
     pp, ep = lax.axis_index("pp"), lax.axis_index("ep")
     zh, y, c = ep // 16, (ep // 2) % N_Y, ep % 2
     oz = 1 - zh
+    side = 2 * (y % 2) - 1
+    other = y - side
 
     def at(rank, z, row, core):
         return {"pp": rank, "ep": z * 16 + row * 2 + core}
@@ -105,25 +107,38 @@
     def send_z(k):
         return copy(packed.at[k, pl.ds(2 * oz, 2)], zr.at[k], z_s.at[k], z_r.at[k], at(pp, oz, y, c))
 
-    def send_ya(k, shift):
-        row = row_at(shift)
+    def handler(j):
+        return row_at(N_Y + (side, -2 * side, 3 * side)[j - 1])
+
+    def handled(j):
+        return row_at(N_Y + side * j)
+
+    def send_ya(k, j):
+        row = handler(j)
         return copy(
             packed.at[k, 2 * zh + row // 4], rrecv.at[k, y, 0],
-            ya_s.at[k, shift - 1], ya_r.at[k, shift - 1], at(pp, zh, row, c),
+            ya_s.at[k, j - 1], ya_r.at[k, j - 1], at(pp, zh, row, c),
         )
 
-    def send_yb(k, shift):
-        row = row_at(shift)
+    def send_yb(k, j):
+        row = handler(j)
         return copy(
             zr.at[k, row // 4], rrecv.at[k, y, 1],
-            yb_s.at[k, shift - 1], yb_r.at[k, shift - 1], at(pp, zh, row, c),
+            yb_s.at[k, j - 1], yb_r.at[k, j - 1], at(pp, zh, row, c),
         )
 
-    def send_back(k, shift):
-        row = row_at(shift)
+    def send_on(k, j):
+        rows = rrecv.at[k, handled(j)]
+        return copy(rows, rows, on_s.at[k, j], on_r.at[k, j], at(pp, zh, other, c))
+
+    def send_half(k, j):
+        row = lax.rem(other - side * j + N_Y, N_Y)
+        return copy(osend.at[k, row], half.at[k, j], half_s.at[k, j], half_r.at[k, j], at(pp, zh, other, c))
+
+    def send_back(k, j):
         return copy(
-            osend.at[k, row], frecv.at[k, y],
-            ret_s.at[k, shift - 1], ret_r.at[k, shift - 1], at(pp, zh, row, c),
+            rsend.at[k, j - 1], frecv.at[k, y // 2],
+            ret_s.at[k, j - 1], ret_r.at[k, j - 1], at(pp, zh, handled(j), c),
         )
 
     def send_x(k, d):
@@ -162,7 +177,7 @@
     for w in local:
         w.start()
     barrier = pltpu.get_barrier_semaphore()
-    peers = [at(pp, zh, row_at(shift), c) for shift in range(1, N_Y)]
+    peers = [at(pp, zh, row_at(shift), c) for shift in (1, 2, 3, 5, 6, 7)]
     peers += [at(pp, oz, y, c), at(pp, zh, y, 1 - c)]
     for rank in (next_rank(0), next_rank(1)):
         peers += [at(rank, zh, y, c), at(rank, oz, y, c)]
@@ -263,8 +278,8 @@
         if first:
             enter()
         send_z(k).start()
-        for shift in range(1, N_Y):
-            send_ya(k, shift).start()
+        for j in (3, 2, 1):
+            send_ya(k, j).start()
         rrecv[k, y, 0] = packed[k, 2 * zh + y // 4]
         if first:
             constants()
@@ -272,8 +287,8 @@
     def relay(s, d):
         k = 2 * s + d
         send_z(k).wait_recv()
-        for shift in range(1, N_Y):
-            send_yb(k, shift).start()
+        for j in (3, 2, 1):
+            send_yb(k, j).start()
         rrecv[k, y, 1] = zr[k, y // 4]
 
     def router_hop(k):
@@ -333,10 +348,8 @@
 
     def experts(s, d):
         k = 2 * s + d
-        for shift in range(1, N_Y):
-            send_ya(k, shift).wait_recv()
-        for shift in range(1, N_Y):
-            send_yb(k, shift).wait_recv()
+        for j in range(4):
+            send_on(k, j).wait_recv()
         ubuf[...] = dot(perm[...], rrecv[k].reshape(ROWS, QW)).astype(BF16)
         both = jnp.zeros((TOKS, 4 * HID), F32)
         for q in range(N_Q):
@@ -346,19 +359,35 @@
         for q in range(N_Q):
             obuf[pl.ds(q * TOKS, TOKS)] = dot(hidden, wd[:, pl.ds(q * QW, QW)]).astype(BF16)
         osend[k] = dot(perm_t[...], obuf[...]).astype(BF16).reshape(N_Y, 2, UNIT, QW)
-        for shift in range(1, N_Y):
-            send_back(k, shift).start()
-        frecv[k, y] = osend[k, y]
+        for j in (3, 2, 1, 0):
+            send_half(k, j).start()
+
+    def forward(s, d):
+        k = 2 * s + d
+        for j in (1, 2, 3):
+            send_ya(k, j).wait_recv()
+            send_yb(k, j).wait_recv()
+        for j in range(4):
+            send_on(k, j).start()
+
+    def reduce_pair(s, d):
+        k = 2 * s + d
+        for j in (3, 2, 1, 0):
+            send_half(k, j).wait_recv()
+            total = (osend[k, handled(j)].astype(F32) + half[k, j].astype(F32)).astype(BF16)
+            if j:
+                rsend[k, j - 1] = total
+                send_back(k, j).start()
+            else:
+                frecv[k, y // 2] = total
 
     def finish(s, d):
         k = 2 * s + d
-        for shift in range(1, N_Y):
-            send_back(k, shift).wait_recv()
+        for j in (1, 2, 3):
+            send_back(k, j).wait_recv()
         for zs in range(2):
             for e in range(2):
-                total = frecv[k, 4 * e, zs].astype(F32)
-                for i in range(1, 4):
-                    total = total + frecv[k, 4 * e + i, zs].astype(F32)
+                total = frecv[k, 2 * e, zs].astype(F32) + frecv[k, 2 * e + 1, zs].astype(F32)
                 ssend[k, zs, e] = total.astype(BF16)
         for sums in send_sums(k, d):
             sums.start()
@@ -369,6 +398,8 @@
 
         @pl.when(d == 0)
         def _():
+            reduce_pair(s, 1)
+            at_start(s, True, first_gates)
             gate_table(s, 1)
 
         @pl.when((s < STEPS - 1) & (d == 1))
@@ -383,10 +414,21 @@
             dispatch(k, d, squares)
 
     def mlp(s, d):
+        forward(s, d)
+
+        @pl.when(d == 1)
+        def _():
+            pl.when(s > 0)(lambda: gate_table(s, 0))
+            reduce_pair(s, 0)
+
         at_start(s, d == 0, wait_weights)
         experts(s, d)
 
         at_start(s, d == 0, lambda: router_hop(3))
+
+    def first_gates():
+        order_router()
+        gate_table(0, 0)
 
     def wait_weights():
         for w in local:
@@ -407,8 +449,6 @@
         send_x(2 * s + 1, 1).start()
         at_start(s, True, lambda: router_hop(2))
         twice(mlp, s)
-        at_start(s, True, order_router)
-        gate_table(s, 0)
         twice(results, s)
         return carry
 
@@ -443,10 +483,13 @@
     def drain(k, carry):
         d = lax.rem(k, 2)
         send_z(k).wait_send()
-        for shift in range(1, N_Y):
-            send_ya(k, shift).wait_send()
-            send_yb(k, shift).wait_send()
-            send_back(k, shift).wait_send()
+        for j in range(4):
+            send_on(k, j).wait_send()
+            send_half(k, j).wait_send()
+        for j in (1, 2, 3):
+            send_ya(k, j).wait_send()
+            send_yb(k, j).wait_send()
+            send_back(k, j).wait_send()
         send_x(k, d).wait_send()
         for sums in send_sums(k, d):
             sums.wait_send()
@@ -470,7 +513,9 @@
         ((K, 2, UNIT, QW), BF16),
         ((K, N_Y, 2, UNIT, QW), BF16),
         ((K, N_Y, 2, UNIT, QW), BF16),
-        ((K, N_Y, 2, UNIT, QW), BF16),
+        ((K, 4, 2, UNIT, QW), BF16),
+        ((K, 3, 2, UNIT, QW), BF16),
+        ((K, 4, 2, UNIT, QW), BF16),
         ((K, 2, 2, UNIT, QW), BF16),
         ((K + 2, 4, UNIT, QW), BF16),
         ((K, TOKS, 128), BF16),
@@ -488,7 +533,7 @@
     ]
     semaphores = [
         (2, N_Q), (3,), (3,), (3,), (10,), (10,),
-        (K, 7), (K, 7), (K, 7), (K, 7), (K, 7), (K, 7),
+        (K, 3), (K, 3), (K, 3), (K, 3), (K, 3), (K, 3), (K, 4), (K, 4), (K, 4), (K, 4),
         (K,), (K,), (K,), (K,), (K, 2), (K, 2), (K,), (K,),
     ]
     return pl.pallas_call(

time: 173 us -> 185 us (1.069)
  the two profiles are of different devices: /device:TPU:2 before, /device:TPU:4 now
where the time goes in v4:
time: 185 us
  Pallas kernels  182 us (98%)
  local copies, waits for them, and re-layouts  2.64 us (1%)
    pallas_call x1, Pallas kernels, body(): pl.pallas_call(kernel, out_shape=[jax.ShapeDtypeStruct(rising.shape, BF16...  182 us

profile of v4, /device:TPU:4, one launch (start us, length us, event | category | flops | bytes accessed | tf_op | source)
XLA Modules:
  0.0 185.0 jit_solution(4977733266263169578)
XLA Ops:
  0.6 181.7 %moe_relay.1 = (bf16[1,64,3584]{2,1,0:T(8,128)(2,1)}, bf16[1,64,3584]{2,1,0:T(8,128)(2,1)}) custom-call(bf16[1,64,3584]{2,1,0:T(8,128)(2,1)} %xr_in.1, bf16[1,64,3584]{2,1,0:T(8,128)(2,1)} %xf_in.1, s32[3,1,8,64]{3,2,1,0:T(8,128)} %bitcast.2, s32[3,1,8,64]{3,2,1,0:T(8,128)} %bitcast.3, f32[1,3584]{1,0:T(1,128)} %gain.1, bf16[1,8,3584]{2,1,0:T(8,128)(2,1)} %router.1, ...), custom_call_target="tpu_custom_call" | custom-call | tf_op jit(solution)/shard_map/moe_relay/pallas_call | solution.py:539
  182.4 0.0 copy-start
  182.4 1.9 %copy.13 = bf16[1,64,3584]{2,1,0:T(8,128)(2,1)} copy(bf16[1,64,3584]{2,1,0:T(8,128)(2,1)} %get-tuple-element.4) | data formatting | bytes 917504
  184.2 0.0 copy-done
  184.2 0.8 copy.14
Async XLA Ops:
  182.4 1.9 %copy-start = (bf16[1,64,3584]{2,1,0:T(8,128)(2,1)S(1)}, bf16[1,64,3584]{2,1,0:T(8,128)(2,1)}, u32[]{:S(2)}) copy-start(bf16[1,64,3584]{2,1,0:T(8,128)(2,1)} %get-tuple-element.5) | copy-start | bytes 1376260

commit v5 on v3

--- a/solution.py
+++ b/solution.py
@@ -19,6 +19,7 @@
 D = 3584
 QW = D // N_Q
 ROWS = N_Q * TOKS
+FAR_FIRST = (4, 3, 5, 2, 6, 1, 7)
 UNIT = N_Q * CAP
 HID = 128
 EXPERTS = 256
@@ -85,22 +86,19 @@
         ]
         return local, remote
 
-    def router_pair():
-        return copy(rown, rgath.at[y, 0, 0], rt_s.at[9], rt_r.at[9], at(pp, zh, y, 1))
-
     def router_z():
-        return copy(rgath.at[y, 0], rgath.at[y, 1], rt_s.at[0], rt_r.at[0], at(pp, oz, y, 1))
+        return copy(rown, rgath.at[0, y, 1], rt_s.at[0], rt_r.at[0], at(pp, oz, y, c))
 
     def router_right(k):
-        block = rgath.at[row_at(N_Y - k)]
-        return copy(block, block, rt_s.at[1 + k], rt_r.at[1 + k], at(pp, zh, row_at(1), 1))
+        block = rgath.at[0, row_at(N_Y - k)]
+        return copy(block, block, rt_s.at[1 + k], rt_r.at[1 + k], at(pp, zh, row_at(1), c))
 
     def router_left(k):
-        block = rgath.at[row_at(k)]
-        return copy(block, block, rt_s.at[5 + k], rt_r.at[5 + k], at(pp, zh, row_at(N_Y - 1), 1))
+        block = rgath.at[0, row_at(k)]
+        return copy(block, block, rt_s.at[5 + k], rt_r.at[5 + k], at(pp, zh, row_at(N_Y - 1), c))
 
     def router_core():
-        return copy(rgath, rgath, rt_s.at[8], rt_r.at[8], at(pp, zh, y, 0))
+        return copy(rgath.at[0], rgath.at[1], rt_s.at[8], rt_r.at[8], at(pp, zh, y, 1 - c))
 
     def send_z(k):
         return copy(packed.at[k, pl.ds(2 * oz, 2)], zr.at[k], z_s.at[k], z_r.at[k], at(pp, oz, y, c))
@@ -175,10 +173,7 @@
     own = router[0].astype(F32)
     own = jnp.concatenate([own[:, :HALF], own[:, HALF:]], axis=0).astype(BF16)
     rown[...] = own
-
-    @pl.when(c == 1)
-    def _():
-        rgath[y, 0, 1] = own
+    rgath[0, y, 0] = own
 
     for load in loads[:N_Q]:
         load.wait()
@@ -231,10 +226,7 @@
 
     def enter():
         pl.semaphore_wait(barrier, len(peers))
-
-        @pl.when(c == 0)
-        def _():
-            router_pair().start()
+        router_z().start()
 
     def constants():
         for w in remote:
@@ -246,11 +238,6 @@
         perm_t[...] = one_hot(
             ((r % 64) // 4 == u // 16) & (r // 64 == (u // 4) % 4) & (r % 4 == u % 4)
         )
-
-        @pl.when(c == 1)
-        def _():
-            router_pair().wait_recv()
-            router_z().start()
 
     def dispatch(k, d, squares, first=False):
         inverse = lax.rsqrt(squares * (1.0 / D) + norm_eps)
@@ -263,7 +250,7 @@
         if first:
             enter()
         send_z(k).start()
-        for shift in range(1, N_Y):
+        for shift in FAR_FIRST:
             send_ya(k, shift).start()
         rrecv[k, y, 0] = packed[k, 2 * zh + y // 4]
         if first:
@@ -272,36 +259,29 @@
     def relay(s, d):
         k = 2 * s + d
         send_z(k).wait_recv()
-        for shift in range(1, N_Y):
+        for shift in FAR_FIRST:
             send_yb(k, shift).start()
         rrecv[k, y, 1] = zr[k, y // 4]
 
     def router_hop(k):
-        @pl.when(c == 1)
-        def _():
-            if k == 0:
-                router_z().wait_recv()
-            else:
-                router_right(k - 1).wait_recv()
-            if k < 4:
-                router_right(k).start()
-            if 0 < k < 4:
-                router_left(k - 1).wait_recv()
-            if k < 3:
-                router_left(k).start()
-            if k == 4:
-                router_core().start()
+        if k == 0:
+            router_z().wait_recv()
+        else:
+            router_right(k - 1).wait_recv()
+        if k < 4:
+            router_right(k).start()
+        if 0 < k < 4:
+            router_left(k - 1).wait_recv()
+        if k < 3:
+            router_left(k).start()
 
     def order_router():
         router_hop(4)
-
-        @pl.when(c == 0)
-        def _():
-            router_core().wait_recv()
-
+        router_core().start()
+        router_core().wait_recv()
         n, row = iota((EXPERTS, 2 * EXPERTS), 0), iota((EXPERTS, 2 * EXPERTS), 1)
-        core, place = (row // 16) % 2, row // 64
-        z = ((row // 32) % 2 + zh) % 2
+        core, place = (row // 256 + c) % 2, (row // 32) % 8
+        z = ((row // 16) % 2 + zh) % 2
         expert = (z * 16 + place * 2 + core) * 8 + row % 8
         for h in range(2):
             pick = one_hot((expert == n) & ((row // 8) % 2 == h))
@@ -346,7 +326,7 @@
         for q in range(N_Q):
             obuf[pl.ds(q * TOKS, TOKS)] = dot(hidden, wd[:, pl.ds(q * QW, QW)]).astype(BF16)
         osend[k] = dot(perm_t[...], obuf[...]).astype(BF16).reshape(N_Y, 2, UNIT, QW)
-        for shift in range(1, N_Y):
+        for shift in FAR_FIRST:
             send_back(k, shift).start()
         frecv[k, y] = osend[k, y]
 
@@ -354,14 +334,14 @@
         k = 2 * s + d
         for shift in range(1, N_Y):
             send_back(k, shift).wait_recv()
-        for zs in range(2):
+        sums = send_sums(k, d)
+        for zs in (1, 0):
             for e in range(2):
                 total = frecv[k, 4 * e, zs].astype(F32)
                 for i in range(1, 4):
                     total = total + frecv[k, 4 * e + i, zs].astype(F32)
                 ssend[k, zs, e] = total.astype(BF16)
-        for sums in send_sums(k, d):
-            sums.start()
+            sums[zs].start()
 
     def results(s, d):
         k = 2 * s + 2 + d
@@ -426,19 +406,12 @@
 
     for w in remote:
         w.wait_send()
-
-    @pl.when(c == 0)
-    def _():
-        router_pair().wait_send()
-
-    @pl.when(c == 1)
-    def _():
-        router_z().wait_send()
-        for k in range(4):
-            router_right(k).wait_send()
-        for k in range(3):
-            router_left(k).wait_send()
-        router_core().wait_send()
+    router_z().wait_send()
+    for k in range(4):
+        router_right(k).wait_send()
+    for k in range(3):
+        router_left(k).wait_send()
+    router_core().wait_send()
 
     def drain(k, carry):
         d = lax.rem(k, 2)
@@ -483,11 +456,11 @@
         ((ROWS, ROWS), BF16),
         ((ROWS, ROWS), BF16),
         ((16, HALF), BF16),
-        ((N_Y, 2, 2, 16, HALF), BF16),
+        ((2, N_Y, 2, 16, HALF), BF16),
         ((N_Q, EXPERTS, QW), BF16),
     ]
     semaphores = [
-        (2, N_Q), (3,), (3,), (3,), (10,), (10,),
+        (2, N_Q), (3,), (3,), (3,), (9,), (9,),
         (K, 7), (K, 7), (K, 7), (K, 7), (K, 7), (K, 7),
         (K,), (K,), (K,), (K,), (K, 2), (K, 2), (K,), (K,),
     ]

time: 173 us -> 170 us (0.983)
  Pallas kernels: 169 us -> 167 us
    pallas_call x1, Pallas kernels: 169 us -> 167 us  [body(): pl.pallas_call(kernel, out_shape=[jax.ShapeDtypeStruct(rising.shape, BF16...]
where the time goes in v5:
time: 170 us
  Pallas kernels  167 us (98%)
  local copies, waits for them, and re-layouts  2.64 us (2%)
    pallas_call x1, Pallas kernels, body(): pl.pallas_call(kernel, out_shape=[jax.ShapeDtypeStruct(rising.shape, BF16...  167 us

profile of v5, /device:TPU:2, one launch (start us, length us, event | category | flops | bytes accessed | tf_op | source)
XLA Modules:
  0.0 170.1 jit_solution(11348421814499895707)
XLA Ops:
  0.6 166.9 %moe_relay.1 = (bf16[1,64,3584]{2,1,0:T(8,128)(2,1)}, bf16[1,64,3584]{2,1,0:T(8,128)(2,1)}) custom-call(bf16[1,64,3584]{2,1,0:T(8,128)(2,1)} %xr_in.1, bf16[1,64,3584]{2,1,0:T(8,128)(2,1)} %xf_in.1, s32[3,1,8,64]{3,2,1,0:T(8,128)} %bitcast.2, s32[3,1,8,64]{3,2,1,0:T(8,128)} %bitcast.3, f32[1,3584]{1,0:T(1,128)} %gain.1, bf16[1,8,3584]{2,1,0:T(8,128)(2,1)} %router.1, ...), custom_call_target="tpu_custom_call" | custom-call | tf_op jit(solution)/shard_map/moe_relay/pallas_call | solution.py:467
  167.5 0.0 copy-start
  167.5 1.9 %copy.13 = bf16[1,64,3584]{2,1,0:T(8,128)(2,1)} copy(bf16[1,64,3584]{2,1,0:T(8,128)(2,1)} %get-tuple-element.4) | data formatting | bytes 917504
  169.4 0.0 copy-done
  169.4 0.8 copy.14
Async XLA Ops:
  167.5 1.9 %copy-start = (bf16[1,64,3584]{2,1,0:T(8,128)(2,1)S(1)}, bf16[1,64,3584]{2,1,0:T(8,128)(2,1)}, u32[]{:S(2)}) copy-start(bf16[1,64,3584]{2,1,0:T(8,128)(2,1)} %get-tuple-element.5) | copy-start | bytes 1376260

commit v6 on v5

--- a/solution.py
+++ b/solution.py
@@ -19,6 +19,7 @@
 D = 3584
 QW = D // N_Q
 ROWS = N_Q * TOKS
+PART = ROWS // 2
 FAR_FIRST = (4, 3, 5, 2, 6, 1, 7)
 UNIT = N_Q * CAP
 HID = 128
@@ -51,7 +52,7 @@
     x, ids, normed, packed, zr, rrecv, osend, frecv, ssend, srecv, gsend, grecv,
     ubuf, obuf, acc, wgu, wd, perm, perm_t, rown, rgath, rall,
     sem_in, sem_w, ws_s, ws_r, rt_s, rt_r,
-    ya_s, ya_r, yb_s, yb_r, ret_s, ret_r, z_s, z_r, x_s, x_r, s_s, s_r, g_s, g_r,
+    y_s, y_r, ret_s, ret_r, z_s, z_r, x_s, x_r, s_s, s_r, g_s, g_r,
 ):
     pp, ep = lax.axis_index("pp"), lax.axis_index("ep")
     zh, y, c = ep // 16, (ep // 2) % N_Y, ep % 2
@@ -103,25 +104,23 @@
     def send_z(k):
         return copy(packed.at[k, pl.ds(2 * oz, 2)], zr.at[k], z_s.at[k], z_r.at[k], at(pp, oz, y, c))
 
+    def send_y(k, part, shift, rows):
+        return copy(
+            rows, rrecv.at[k, y, part],
+            y_s.at[k, part, shift - 1], y_r.at[k, part, shift - 1], at(pp, zh, row_at(shift), c),
+        )
+
     def send_ya(k, shift):
+        return send_y(k, 0, shift, packed.at[k, 2 * zh + row_at(shift) // 4])
+
+    def send_yb(k, shift):
+        return send_y(k, 1, shift, zr.at[k, row_at(shift) // 4])
+
+    def send_back(k, part, shift):
         row = row_at(shift)
         return copy(
-            packed.at[k, 2 * zh + row // 4], rrecv.at[k, y, 0],
-            ya_s.at[k, shift - 1], ya_r.at[k, shift - 1], at(pp, zh, row, c),
-        )
-
-    def send_yb(k, shift):
-        row = row_at(shift)
-        return copy(
-            zr.at[k, row // 4], rrecv.at[k, y, 1],
-            yb_s.at[k, shift - 1], yb_r.at[k, shift - 1], at(pp, zh, row, c),
-        )
-
-    def send_back(k, shift):
-        row = row_at(shift)
-        return copy(
-            osend.at[k, row], frecv.at[k, y],
-            ret_s.at[k, shift - 1], ret_r.at[k, shift - 1], at(pp, zh, row, c),
+            osend.at[k, row, part], frecv.at[k, y, part],
+            ret_s.at[k, part, shift - 1], ret_r.at[k, part, shift - 1], at(pp, zh, row, c),
         )
 
     def send_x(k, d):
@@ -231,12 +230,12 @@
     def constants():
         for w in remote:
             w.start()
-        u, r = iota((ROWS, ROWS), 0), iota((ROWS, ROWS), 1)
+        u, r = iota((PART, PART), 0), iota((PART, PART), 1)
         perm[...] = one_hot(
-            ((u % 64) // 4 == r // 16) & (u // 64 == (r // 4) % 4) & (u % 4 == r % 4)
+            ((u % 32) // 4 == r // 16) & (u // 32 == (r // 4) % 4) & (u % 4 == r % 4)
         )
         perm_t[...] = one_hot(
-            ((r % 64) // 4 == u // 16) & (r // 64 == (u // 4) % 4) & (r % 4 == u % 4)
+            ((r % 32) // 4 == u // 16) & (r // 32 == (u // 4) % 4) & (r % 4 == u % 4)
         )
 
     def dispatch(k, d, squares, first=False):
@@ -313,29 +312,32 @@
 
     def experts(s, d):
         k = 2 * s + d
-        for shift in range(1, N_Y):
-            send_ya(k, shift).wait_recv()
-        for shift in range(1, N_Y):
-            send_yb(k, shift).wait_recv()
-        ubuf[...] = dot(perm[...], rrecv[k].reshape(ROWS, QW)).astype(BF16)
-        both = jnp.zeros((TOKS, 4 * HID), F32)
-        for q in range(N_Q):
-            both = both + dot(ubuf[pl.ds(q * TOKS, TOKS)], wgu[pl.ds(q * QW, QW)])
-        gate, up = both[:, : 2 * HID], both[:, 2 * HID :]
-        hidden = (gate * jax.nn.sigmoid(gate) * up).astype(BF16)
-        for q in range(N_Q):
-            obuf[pl.ds(q * TOKS, TOKS)] = dot(hidden, wd[:, pl.ds(q * QW, QW)]).astype(BF16)
-        osend[k] = dot(perm_t[...], obuf[...]).astype(BF16).reshape(N_Y, 2, UNIT, QW)
-        for shift in FAR_FIRST:
-            send_back(k, shift).start()
-        frecv[k, y] = osend[k, y]
+
+        def one(part, carry):
+            for shift in range(1, N_Y):
+                send_y(k, part, shift, zr.at[k, 0]).wait_recv()
+            ubuf[...] = dot(perm[...], rrecv[k, :, part].reshape(PART, QW)).astype(BF16)
+            both = jnp.zeros((32, 4 * HID), F32)
+            for q in range(N_Q):
+                both = both + dot(ubuf[pl.ds(q * 32, 32)], wgu[pl.ds(q * QW, QW)])
+            gate, up = both[:, : 2 * HID], both[:, 2 * HID :]
+            hidden = (gate * jax.nn.sigmoid(gate) * up).astype(BF16)
+            for q in range(N_Q):
+                obuf[pl.ds(q * 32, 32)] = dot(hidden, wd[:, pl.ds(q * QW, QW)]).astype(BF16)
+            osend[k, :, part] = dot(perm_t[...], obuf[...]).astype(BF16).reshape(N_Y, UNIT, QW)
+            for shift in FAR_FIRST:
+                send_back(k, part, shift).start()
+            frecv[k, y, part] = osend[k, y, part]
+            return carry
+
+        lax.fori_loop(0, 2, one, 0)
 
     def finish(s, d):
         k = 2 * s + d
-        for shift in range(1, N_Y):
-            send_back(k, shift).wait_recv()
         sums = send_sums(k, d)
-        for zs in (1, 0):
+        for zs in range(2):
+            for shift in range(1, N_Y):
+                send_back(k, zs, shift).wait_recv()
             for e in range(2):
                 total = frecv[k, 4 * e, zs].astype(F32)
                 for i in range(1, 4):
@@ -419,7 +421,8 @@
         for shift in range(1, N_Y):
             send_ya(k, shift).wait_send()
             send_yb(k, shift).wait_send()
-            send_back(k, shift).wait_send()
+            send_back(k, 0, shift).wait_send()
+            send_back(k, 1, shift).wait_send()
         send_x(k, d).wait_send()
         for sums in send_sums(k, d):
             sums.wait_send()
@@ -448,20 +451,20 @@
         ((K + 2, 4, UNIT, QW), BF16),
         ((K, TOKS, 128), BF16),
         ((K + 2, TOKS, 128), BF16),
-        ((ROWS, QW), BF16),
-        ((ROWS, QW), BF16),
+        ((PART, QW), BF16),
+        ((PART, QW), BF16),
         ((ROWS, QW), F32),
         ((D, 4 * HID), BF16),
         ((2 * HID, D), BF16),
-        ((ROWS, ROWS), BF16),
-        ((ROWS, ROWS), BF16),
+        ((PART, PART), BF16),
+        ((PART, PART), BF16),
         ((16, HALF), BF16),
         ((2, N_Y, 2, 16, HALF), BF16),
         ((N_Q, EXPERTS, QW), BF16),
     ]
     semaphores = [
         (2, N_Q), (3,), (3,), (3,), (9,), (9,),
-        (K, 7), (K, 7), (K, 7), (K, 7), (K, 7), (K, 7),
+        (K, 2, 7), (K, 2, 7), (K, 2, 7), (K, 2, 7),
         (K,), (K,), (K,), (K,), (K, 2), (K, 2), (K,), (K,),
     ]
     return pl.pallas_call(

time: 170 us -> 170 us (level)
  the two profiles are of different devices: /device:TPU:2 before, /device:TPU:1 now
where the time goes in v6:
time: 170 us
  Pallas kernels  167 us (98%)
  local copies, waits for them, and re-layouts  2.64 us (2%)
    pallas_call x1, Pallas kernels, body(): pl.pallas_call(kernel, out_shape=[jax.ShapeDtypeStruct(rising.shape, BF16...  167 us

profile of v6, /device:TPU:1, one launch (start us, length us, event | category | flops | bytes accessed | tf_op | source)
XLA Modules:
  0.0 170.1 jit_solution(12093975950837829741)
XLA Ops:
  0.6 166.8 %moe_relay.1 = (bf16[1,64,3584]{2,1,0:T(8,128)(2,1)}, bf16[1,64,3584]{2,1,0:T(8,128)(2,1)}) custom-call(bf16[1,64,3584]{2,1,0:T(8,128)(2,1)} %xr_in.1, bf16[1,64,3584]{2,1,0:T(8,128)(2,1)} %xf_in.1, s32[3,1,8,64]{3,2,1,0:T(8,128)} %bitcast.2, s32[3,1,8,64]{3,2,1,0:T(8,128)} %bitcast.3, f32[1,3584]{1,0:T(1,128)} %gain.1, bf16[1,8,3584]{2,1,0:T(8,128)(2,1)} %router.1, ...), custom_call_target="tpu_custom_call" | custom-call | tf_op jit(solution)/shard_map/moe_relay/pallas_call | solution.py:470
  167.4 0.0 copy-start
  167.4 1.9 %copy.13 = bf16[1,64,3584]{2,1,0:T(8,128)(2,1)} copy(bf16[1,64,3584]{2,1,0:T(8,128)(2,1)} %get-tuple-element.4) | data formatting | bytes 917504
  169.3 0.0 copy-done
  169.3 0.8 copy.14
Async XLA Ops:
  167.4 1.9 %copy-start = (bf16[1,64,3584]{2,1,0:T(8,128)(2,1)S(1)}, bf16[1,64,3584]{2,1,0:T(8,128)(2,1)}, u32[]{:S(2)}) copy-start(bf16[1,64,3584]{2,1,0:T(8,128)(2,1)} %get-tuple-element.5) | copy-start | bytes 1376260

commit v7 on v6

--- a/solution.py
+++ b/solution.py
@@ -50,7 +50,7 @@
     xr_in, xf_in, idr_in, idf_in, gain, router, wg_in, wu_in, wd_in,
     outr, outf,
     x, ids, normed, packed, zr, rrecv, osend, frecv, ssend, srecv, gsend, grecv,
-    ubuf, obuf, acc, wgu, wd, perm, perm_t, rown, rgath, rall,
+    ubuf, obuf, acc, wgu, wd, perm, perm_t, rgath, rall,
     sem_in, sem_w, ws_s, ws_r, rt_s, rt_r,
     y_s, y_r, ret_s, ret_r, z_s, z_r, x_s, x_r, s_s, s_r, g_s, g_r,
 ):
@@ -87,19 +87,20 @@
         ]
         return local, remote
 
-    def router_z():
-        return copy(rown, rgath.at[0, y, 1], rt_s.at[0], rt_r.at[0], at(pp, oz, y, c))
+    def router_z(i):
+        row = row_at(N_Y - i) if i <= 4 else row_at(i - 4)
+        return copy(rgath.at[0, row, 0], rgath.at[0, row, 1], rt_s.at[i], rt_r.at[i], at(pp, oz, y, c))
 
     def router_right(k):
-        block = rgath.at[0, row_at(N_Y - k)]
-        return copy(block, block, rt_s.at[1 + k], rt_r.at[1 + k], at(pp, zh, row_at(1), c))
+        block = rgath.at[0, row_at(N_Y - k), 0]
+        return copy(block, block, rt_s.at[8 + k], rt_r.at[8 + k], at(pp, zh, row_at(1), c))
 
     def router_left(k):
-        block = rgath.at[0, row_at(k)]
-        return copy(block, block, rt_s.at[5 + k], rt_r.at[5 + k], at(pp, zh, row_at(N_Y - 1), c))
+        block = rgath.at[0, row_at(k), 0]
+        return copy(block, block, rt_s.at[12 + k], rt_r.at[12 + k], at(pp, zh, row_at(N_Y - 1), c))
 
     def router_core():
-        return copy(rgath.at[0], rgath.at[1], rt_s.at[8], rt_r.at[8], at(pp, zh, y, 1 - c))
+        return copy(rgath.at[0], rgath.at[1], rt_s.at[15], rt_r.at[15], at(pp, zh, y, 1 - c))
 
     def send_z(k):
         return copy(packed.at[k, pl.ds(2 * oz, 2)], zr.at[k], z_s.at[k], z_r.at[k], at(pp, oz, y, c))
@@ -171,7 +172,6 @@
         ids[2 * s + 1] = idf_in[s, 0].T
     own = router[0].astype(F32)
     own = jnp.concatenate([own[:, :HALF], own[:, HALF:]], axis=0).astype(BF16)
-    rown[...] = own
     rgath[0, y, 0] = own
 
     for load in loads[:N_Q]:
@@ -225,7 +225,8 @@
 
     def enter():
         pl.semaphore_wait(barrier, len(peers))
-        router_z().start()
+        router_z(0).start()
+        router_hop(0)
 
     def constants():
         for w in remote:
@@ -263,19 +264,20 @@
         rrecv[k, y, 1] = zr[k, y // 4]
 
     def router_hop(k):
-        if k == 0:
-            router_z().wait_recv()
-        else:
+        if k:
             router_right(k - 1).wait_recv()
+            router_z(k).start()
         if k < 4:
             router_right(k).start()
         if 0 < k < 4:
             router_left(k - 1).wait_recv()
+            router_z(4 + k).start()
         if k < 3:
             router_left(k).start()
 
     def order_router():
-        router_hop(4)
+        for i in range(8):
+            router_z(i).wait_recv()
         router_core().start()
         router_core().wait_recv()
         n, row = iota((EXPERTS, 2 * EXPERTS), 0), iota((EXPERTS, 2 * EXPERTS), 1)
@@ -368,7 +370,7 @@
         at_start(s, d == 0, wait_weights)
         experts(s, d)
 
-        at_start(s, d == 0, lambda: router_hop(3))
+        at_start(s, d == 0, lambda: router_hop(4))
 
     def wait_weights():
         for w in local:
@@ -387,7 +389,7 @@
         relay(s, 1)
         send_x(2 * s, 0).start()
         send_x(2 * s + 1, 1).start()
-        at_start(s, True, lambda: router_hop(2))
+        at_start(s, True, lambda: router_hop(3))
         twice(mlp, s)
         at_start(s, True, order_router)
         gate_table(s, 0)
@@ -395,12 +397,12 @@
         return carry
 
     dispatch(0, 0, first_state(0), first=True)
-    router_hop(0)
+    router_hop(1)
     relay(0, 0)
     for load in loads[N_Q:]:
         load.wait()
     dispatch(1, 1, first_state(1))
-    router_hop(1)
+    router_hop(2)
     lax.fori_loop(0, STEPS, step, 0)
     stores = state_out(0, outr) + state_out(1, outf)
     for store in stores:
@@ -408,7 +410,8 @@
 
     for w in remote:
         w.wait_send()
-    router_z().wait_send()
+    for i in range(8):
+        router_z(i).wait_send()
     for k in range(4):
         router_right(k).wait_send()
     for k in range(3):
@@ -458,12 +461,11 @@
         ((2 * HID, D), BF16),
         ((PART, PART), BF16),
         ((PART, PART), BF16),
-        ((16, HALF), BF16),
         ((2, N_Y, 2, 16, HALF), BF16),
         ((N_Q, EXPERTS, QW), BF16),
     ]
     semaphores = [
-        (2, N_Q), (3,), (3,), (3,), (9,), (9,),
+        (2, N_Q), (3,), (3,), (3,), (16,), (16,),
         (K, 2, 7), (K, 2, 7), (K, 2, 7), (K, 2, 7),
         (K,), (K,), (K,), (K,), (K, 2), (K, 2), (K,), (K,),
     ]

time: 170 us -> 168 us (0.988)
  the two profiles are of different devices: /device:TPU:1 before, /device:TPU:68 now
where the time goes in v7:
time: 168 us
  Pallas kernels  165 us (98%)
  local copies, waits for them, and re-layouts  2.64 us (2%)
    pallas_call x1, Pallas kernels, body(): pl.pallas_call(kernel, out_shape=[jax.ShapeDtypeStruct(rising.shape, BF16...  165 us

profile of v7, /device:TPU:68, one launch (start us, length us, event | category | flops | bytes accessed | tf_op | source)
XLA Modules:
  0.0 168.2 jit_solution(10356137001385771804)
XLA Ops:
  0.6 164.9 %moe_relay.1 = (bf16[1,64,3584]{2,1,0:T(8,128)(2,1)}, bf16[1,64,3584]{2,1,0:T(8,128)(2,1)}) custom-call(bf16[1,64,3584]{2,1,0:T(8,128)(2,1)} %xr_in.1, bf16[1,64,3584]{2,1,0:T(8,128)(2,1)} %xf_in.1, s32[3,1,8,64]{3,2,1,0:T(8,128)} %bitcast.2, s32[3,1,8,64]{3,2,1,0:T(8,128)} %bitcast.3, f32[1,3584]{1,0:T(1,128)} %gain.1, bf16[1,8,3584]{2,1,0:T(8,128)(2,1)} %router.1, ...), custom_call_target="tpu_custom_call" | custom-call | tf_op jit(solution)/shard_map/moe_relay/pallas_call | solution.py:472
  165.6 0.0 copy-start
  165.6 1.9 %copy.13 = bf16[1,64,3584]{2,1,0:T(8,128)(2,1)} copy(bf16[1,64,3584]{2,1,0:T(8,128)(2,1)} %get-tuple-element.4) | data formatting | bytes 917504
  167.4 0.0 copy-done
  167.4 0.8 copy.14
Async XLA Ops:
  165.6 1.9 %copy-start = (bf16[1,64,3584]{2,1,0:T(8,128)(2,1)S(1)}, bf16[1,64,3584]{2,1,0:T(8,128)(2,1)}, u32[]{:S(2)}) copy-start(bf16[1,64,3584]{2,1,0:T(8,128)(2,1)} %get-tuple-element.5) | copy-start | bytes 1376260
